TPU v7x, 32 devices: a whole 2x2x4 slice. The times are simulated.
32 devices in a mesh: tm: 4 (over z), row: 8 (over y, x, core).
Axes of the slice: x: 2, y: 2, z: 4, core: 2. Of those that a mesh axis runs over, the one named last changes fastest.
Arguments:
- solution: float32 [4, 16, 8192], P('tm', None, 'row'), may hold values from -6 to 6
- residual: float32 [4, 16, 8192], P('tm', None, 'row'), may hold values from -6 to 6
- direction: float32 [4, 16, 8192], P('tm', None, 'row'), may hold values from -6 to 6
- normal: bfloat16 [4, 8192, 8192], P('tm', 'row'), as said below
- weights: float32 [8192], P('row'), may hold values from 0.3 to 3
Outputs:
- new_solution: float32 [4, 16, 8192], P('tm', None, 'row')
- new_residual: float32 [4, 16, 8192], P('tm', None, 'row')
- new_direction: float32 [4, 16, 8192], P('tm', None, 'row')
Inputs may be any that keep to these rules, and one draw needn't show every extreme that they name: `normal`: each month's block of 8192 x 8192 is symmetric and positive definite.
All inputs are finite; a program needn't handle non-finite values.
Results may differ from a plain program's by a relative error of at most 0.0026.
Values may be sent and summed in bfloat16 or wider, within the bound.
No kernel may reach another device: no remote copies, remote signals or barrier semaphores. Data moves between devices by JAX's collectives and lax.ppermute only.
A program may use at most 64 MiB of HBM per device.

v0:
```python
import jax
import jax.numpy as jnp
from jax import lax
from jax.sharding import PartitionSpec as P

HIGH = lax.Precision.HIGHEST


def padded_2(cells, sides, width):
    for axis, dim in sides:
        count = lax.axis_size(axis)
        ends = count - 1
        head = lax.slice_in_dim(cells, 0, width, axis=dim)
        tail = lax.slice_in_dim(cells, cells.shape[dim] - width, cells.shape[dim], axis=dim)
        cells = jnp.concatenate(
            [
                lax.ppermute(tail, axis, [(i, (i + 1) % count) for i in range(ends)]),
                cells,
                lax.ppermute(head, axis, [((i + 1) % count, i) for i in range(ends)]),
            ],
            axis=dim,
        )
    return cells


def solve_spd(matrix, rhs):
    lower = jnp.linalg.cholesky(matrix)
    inner = lax.linalg.triangular_solve(lower, rhs, left_side=True, lower=True, transpose_a=False)
    return lax.linalg.triangular_solve(lower, inner, left_side=True, lower=True, transpose_a=True)


def local_gram(left, right):
    return lax.dot_general(
        left, right, (((1,), (1,)), ((), ())), precision=HIGH, preferred_element_type=jnp.float32
    )


def combine(coeffs, block):
    return jnp.dot(coeffs.T, block, precision=HIGH, preferred_element_type=jnp.float32)


def local(solution, residual, direction, normal, weights):
    slab = normal[0]
    dirs = direction[0]
    resid = residual[0]
    dir_low = direction.astype(jnp.bfloat16)
    own_low = dir_low[0]
    product = lax.dot_general(
        lax.all_gather(own_low, "row", axis=1, tiled=True),
        slab,
        (((1,), (1,)), ((), ())),
        preferred_element_type=jnp.float32,
    )
    padded = padded_2(dir_low, (("tm", 0),), 1)
    month_idx = lax.axis_index("tm")
    last_month = lax.axis_size("tm") - 1
    has_prev = (month_idx > 0).astype(jnp.float32)
    has_next = (month_idx < last_month).astype(jnp.float32)
    centre = own_low.astype(jnp.float32)
    coupled = has_prev * (centre - padded[0].astype(jnp.float32)) + has_next * (
        centre - padded[2].astype(jnp.float32)
    )
    image = product + weights[None, :] * coupled
    gram_old = lax.psum(local_gram(resid, resid), ("tm", "row"))
    gram_old = 0.5 * (gram_old + gram_old.T)
    curvature = lax.psum(local_gram(dirs, image), ("tm", "row"))
    curvature = 0.5 * (curvature + curvature.T)
    alpha = solve_spd(curvature, gram_old)
    next_resid = resid - combine(alpha, image)
    gram_new = lax.psum(local_gram(next_resid, next_resid), ("tm", "row"))
    beta = solve_spd(gram_old, gram_new)
    next_solution = solution[0] + combine(alpha, dirs)
    next_direction = next_resid + combine(beta, dirs)
    return (next_solution[None], next_resid[None], next_direction[None])


def solution(mesh):
    placed = (
        P("tm", None, "row"),
        P("tm", None, "row"),
        P("tm", None, "row"),
        P("tm", "row", None),
        P("row"),
    )
    return jax.shard_map(
        local,
        mesh=mesh,
        in_specs=placed,
        out_specs=(P("tm", None, "row"), P("tm", None, "row"), P("tm", None, "row")),
        check_vma=False,
    )
```

profile of v0, /device:TPU:0, one launch (start us, length us, event | category | flops | bytes accessed | tf_op | source)
XLA Modules:
  0.0 121.8 jit_solution(8214001388687501488)
XLA Ops:
  0.6 0.0 copy-start
  0.6 0.0 copy-start.2
  0.7 0.0 copy-start.3
  0.7 0.9 convert_element_type.24
  1.6 4.9 %collective-permute-start = (bf16[1,16,1024]{2,1,0:T(8,128)(2,1)S(1)}, bf16[1,16,1024]{2,1,0:T(8,128)(2,1)S(1)}, u32[]{:S(2)}, u32[]{:S(2)}) collective-permute-start(bf16[1,16,1024]{2,1,0:T(8,128)(2,1)S(1)} %convert_element_type.24), channel_id=1, source_target_pairs={{0,8},{8,16},{16,24},{1,9},{9,17},{17,25},{2,10},{10,18},{18,26},{... | collective-permute-start | bytes 98312 | tf_op jit(solution)/shard_map/ppermute | solution.py:17
  6.5 1.3 %collective-permute-start.1 = (bf16[1,16,1024]{2,1,0:T(8,128)(2,1)S(1)}, bf16[1,16,1024]{2,1,0:T(8,128)(2,1)S(1)}, u32[]{:S(2)}, u32[]{:S(2)}) collective-permute-start(bf16[1,16,1024]{2,1,0:T(8,128)(2,1)S(1)} %convert_element_type.24), channel_id=1, source_target_pairs={{8,0},{16,8},{24,16},{9,1},{17,9},{25,17},{10,2},{18,10},{26,18},{... | collective-permute-start | bytes 98312 | tf_op jit(solution)/shard_map/ppermute | solution.py:19
  7.8 1.1 fusion.13
  8.9 9.3 %all-gather = bf16[1,16,8192]{2,1,0:T(8,128)(2,1)S(1)} all-gather(bf16[1,16,1024]{2,1,0:T(8,128)(2,1)S(1)} %convert_element_type.24), channel_id=2, replica_groups=mesh['tm'=4,'row'=8] {'row'}, dimensions={2}, use_global_device_ids=true | all-gather | bytes 294912 | tf_op jit(solution)/shard_map/all_gather | solution.py:49
  18.2 0.0 collective-permute-done
  18.2 0.0 collective-permute-done.1
  18.2 10.2 %fusion.4 = f32[16,1024]{1,0:T(8,128)S(1)} fusion(bf16[1,1024,8192]{2,1,0:T(8,128)(2,1)} %param.13, bf16[1,16,8192]{2,1,0:T(8,128)(2,1)S(1)} %all-gather, bf16[1,16,1024]{2,1,0:T(8,128)(2,1)S(1)} %convert_element_type.24, bf16[1,16,1024]{2,1,0:T(8,128)(2,1)S(1)} %collective-permute-done.1, bf16[1,16,1024]{2,1,0:T(8,128)(2,1)S(1)} %collective-permute-done, ...), kind=kOutput, calls=%fused_computation.7 | convolution fusion | flops 268599296 | bytes 17207304 | tf_op jit(solution)/shard_map/dot_general | solution.py:48
  28.4 0.0 copy-done
  28.4 0.2 convolution_bitcast_fusion
  28.6 40.8 %all-reduce = (f32[16,16]{1,0:T(8,128)S(1)}, f32[16,16]{1,0:T(8,128)S(1)}) all-reduce(f32[16,16]{1,0:T(8,128)S(1)} %fusion.13, f32[16,16]{1,0:T(8,128)S(1)} %convolution_bitcast_fusion), channel_id=1, replica_groups=mesh['tm'=4,'row'=8] {'tm','row'}, use_global_device_ids=true, to_apply=%region_3.5 | all-reduce | flops 512 | bytes 4096 | tf_op jit(solution)/shard_map/psum | solution.py:64
  69.4 0.1 copy.11
  69.5 0.1 copy.9
  69.6 0.1 copy.12
  69.6 1.5 %cholesky.55 = f32[16,16]{1,0:T(8,128)S(1)} custom-call(f32[16,16]{1,0:T(8,128)S(1)} %fusion.24), custom_call_target="Cholesky" | custom-call | tf_op jit(solution)/shard_map/jit(cholesky)/cholesky | solution.py:27
  71.1 0.6 compare_reduce_fusion
  71.8 0.6 fusion.19
  72.4 1.2 %custom-call.13 = f32[1,16,16]{1,2,0:T(8,128)S(1)} custom-call(f32[1,16,16]{2,1,0:T(8,128)S(1)} %fusion.19), custom_call_target="InvertDiagBlocksLowerTriangular" | custom-call | tf_op jit(solution)/shard_map/triangular_solve/custom-call.2 | solution.py:29
  73.7 0.1 copy.10
  73.7 1.5 %cholesky.44 = f32[16,16]{1,0:T(8,128)S(1)} custom-call(f32[16,16]{1,0:T(8,128)S(1)} %fusion.30), custom_call_target="Cholesky" | custom-call | tf_op jit(solution)/shard_map/jit(cholesky)/cholesky | solution.py:27
  75.2 0.6 compare_reduce_fusion.1
  75.9 0.6 fusion.18
  76.5 1.2 %custom-call.11 = f32[1,16,16]{1,2,0:T(8,128)S(1)} custom-call(f32[1,16,16]{2,1,0:T(8,128)S(1)} %fusion.18), custom_call_target="InvertDiagBlocksLowerTriangular" | custom-call | tf_op jit(solution)/shard_map/triangular_solve/custom-call.2 | solution.py:29
  77.8 0.2 fusion.26
  78.0 0.1 fusion.28
  78.1 0.0 copy-done.2
  78.1 0.3 convolution_subtract_fusion
  78.4 0.0 copy-start.1
  78.4 0.2 fusion.32
  78.6 41.1 %psum.23 = f32[16,16]{1,0:T(8,128)S(1)} all-reduce(f32[16,16]{1,0:T(8,128)S(1)} %fusion.32), channel_id=1, replica_groups=mesh['tm'=4,'row'=8] {'tm','row'}, use_global_device_ids=true, to_apply=%region_4.8 | all-reduce | flops 256 | bytes 2048 | tf_op jit(solution)/shard_map/psum | solution.py:70
  119.6 0.2 fusion.20
  119.8 0.1 fusion.22
  120.0 0.9 fusion.2
  120.9 0.0 copy-done.3
  120.9 0.9 fusion.3
  121.8 0.0 copy-done.1
  (5 shorter events, 0.1 us)
Async XLA Ops:
  0.6 27.8 %copy-start = (f32[1,16,1024]{2,1,0:T(8,128)S(1)}, f32[1,16,1024]{2,1,0:T(8,128)}, u32[]{:S(2)}) copy-start(f32[1,16,1024]{2,1,0:T(8,128)} %param.12) | copy-start | bytes 196612
  0.6 77.5 %copy-start.2 = (f32[1,16,1024]{2,1,0:T(8,128)S(1)}, f32[1,16,1024]{2,1,0:T(8,128)}, u32[]{:S(2)}) copy-start(f32[1,16,1024]{2,1,0:T(8,128)} %param.11) | copy-start | bytes 196612
  0.7 120.2 %copy-start.3 = (f32[1,16,1024]{2,1,0:T(8,128)S(1)}, f32[1,16,1024]{2,1,0:T(8,128)}, u32[]{:S(2)}) copy-start(f32[1,16,1024]{2,1,0:T(8,128)} %param.10) | copy-start | bytes 196612
  1.6 16.7 %collective-permute-start = (bf16[1,16,1024]{2,1,0:T(8,128)(2,1)S(1)}, bf16[1,16,1024]{2,1,0:T(8,128)(2,1)S(1)}, u32[]{:S(2)}, u32[]{:S(2)}) collective-permute-start(bf16[1,16,1024]{2,1,0:T(8,128)(2,1)S(1)} %convert_element_type.24), channel_id=1, source_target_pairs={{0,8},{8,16},{16,24},{1,9},{9,17},{17,25},{2,10},{10,18},{18,26},{... | collective-permute-start | bytes 98312 | tf_op jit(solution)/shard_map/ppermute | solution.py:17
  6.5 11.8 %collective-permute-start.1 = (bf16[1,16,1024]{2,1,0:T(8,128)(2,1)S(1)}, bf16[1,16,1024]{2,1,0:T(8,128)(2,1)S(1)}, u32[]{:S(2)}, u32[]{:S(2)}) collective-permute-start(bf16[1,16,1024]{2,1,0:T(8,128)(2,1)S(1)} %convert_element_type.24), channel_id=1, source_target_pairs={{8,0},{16,8},{24,16},{9,1},{17,9},{25,17},{10,2},{18,10},{26,18},{... | collective-permute-start | bytes 98312 | tf_op jit(solution)/shard_map/ppermute | solution.py:19
  78.4 43.4 %copy-start.1 = (f32[16,1024]{1,0:T(8,128)}, f32[16,1024]{1,0:T(8,128)S(1)}, u32[]{:S(2)}) copy-start(f32[16,1024]{1,0:T(8,128)S(1)} %convolution_subtract_fusion) | copy-start | bytes 196612
where the time goes:
time: 122 us
  blocking collectives  91.2 us (75%)
  matrix products  14.4 us (12%)
  other arithmetic  8.94 us (7%)
  starting transfers between devices  6.21 us (5%)
    psum x1, blocking collectives, local(): gram_new = lax.psum(local_gram(next_resid, next_resid), ('tm', 'row'))  41.1 us
    psum x1, blocking collectives, local(): gram_old = lax.psum(local_gram(resid, resid), ('tm', 'row'))  40.8 us
    dot_general x1, matrix products, local(): lax.dot_general(lax.all_gather(own_low, 'row', axis=1, tiled=True), slab,...  10.2 us
    all_gather x1, blocking collectives, local(): lax.all_gather(own_low, 'row', axis=1, tiled=True)  9.34 us
    ppermute x1, starting transfers between devices, padded_2(): lax.ppermute(tail, axis, [(i, (i + 1) % count) for i in range(ends)])  4.92 us
    another operation x6, other arithmetic, solve_spd(): lower = jnp.linalg.cholesky(matrix)  4.27 us
    another operation x4, other arithmetic, solve_spd(): lax.linalg.triangular_solve(lower, inner, left_side=True, lower=True, tra...  3.75 us
  transfers between devices with their start and end apart: 2, of which 0 were waited for; matrix products, arithmetic and copies ran while one was open for 1% of the time, Pallas kernels for 0%

commit v1 on v0

v1 whole, which is shorter than its diff:
```python
import functools

import jax
import jax.numpy as jnp
from jax import lax
from jax.experimental import pallas as pl
from jax.experimental.pallas import tpu as pltpu
from jax.sharding import PartitionSpec as P

HIGH = lax.Precision.HIGHEST
ROWS_BY_ROWS = (((1,), (1,)), ((), ()))
SMEM = pl.BlockSpec(memory_space=pltpu.SMEM)
VMEM = pl.BlockSpec(memory_space=pltpu.VMEM)
HBM = pl.BlockSpec(memory_space=pltpu.HBM)
TILE = 256


def dot_nt(left, right):
    return lax.dot_general(left, right, ROWS_BY_ROWS, precision=HIGH, preferred_element_type=jnp.float32)


def dot_nn(left, right):
    return jnp.dot(left, right, precision=HIGH, preferred_element_type=jnp.float32)


def round_kernel(wide_ref, low_ref):
    low_ref[...] = wide_ref[...].astype(jnp.bfloat16)


def place_kernel(slots_ref, _, *refs):
    *parts, out_ref = refs
    width = parts[0].shape[1]
    for i, part in enumerate(parts):
        out_ref[:, pl.ds(pl.multiple_of(slots_ref[i] * width, width), width)] = part[...]


def product_of(places_ref, blocks, slab_ref, sum_ref, out_ref):
    rows = slab_ref.shape[0]
    width = blocks[0].shape[1]
    tile = min(TILE, rows)
    for start in range(0, rows, tile):
        part = pl.ds(start, tile)
        total = None if sum_ref is None else sum_ref[:, part]
        for i, block in enumerate(blocks):
            columns = pl.ds(pl.multiple_of(places_ref[i] * width, width), width)
            term = lax.dot_general(
                block[...], slab_ref[part, columns], ROWS_BY_ROWS, preferred_element_type=jnp.float32
            )
            total = term if total is None else total + term
        out_ref[:, part] = total


def first_kernel(places_ref, block_ref, next_ref, low_ref, slab_ref, out_ref, low_out_ref):
    low_out_ref[...] = low_ref[...]
    product_of(places_ref, [block_ref, next_ref], slab_ref, None, out_ref)


def image_kernel(count, places_ref, ends_ref, *refs):
    blocks, refs = refs[:count], refs[count:]
    slab_ref, sum_ref, dirs_ref, resid_ref, before_ref, after_ref, weights_ref = refs[:7]
    image_ref, grams_ref = refs[7:]
    dirs = dirs_ref[...]
    resid = resid_ref[...]
    centre = dirs.astype(jnp.bfloat16).astype(jnp.float32)
    has_prev = ends_ref[0].astype(jnp.float32)
    has_next = ends_ref[1].astype(jnp.float32)
    coupled = has_prev * (centre - before_ref[...].astype(jnp.float32)) + has_next * (
        centre - after_ref[...].astype(jnp.float32)
    )
    image_ref[...] = sum_ref[...] + weights_ref[...] * coupled
    product_of(places_ref, blocks, slab_ref, image_ref, image_ref)
    image = image_ref[...]
    left = jnp.concatenate([resid, dirs, image], axis=0)
    right = jnp.concatenate([resid, image], axis=0)
    grams = dot_nt(left, right)
    rhs = resid.shape[0]
    grams_ref[...] = jnp.concatenate([grams[:rhs], grams[rhs : 2 * rhs], grams[2 * rhs :]], axis=1)


def right_divide(*systems):
    size = systems[0][0].shape[0]
    works = [jnp.concatenate(system, axis=0) for system in systems]
    lane = lax.broadcasted_iota(jnp.int32, works[0].shape, 1)
    for k in range(size):
        for i, work in enumerate(works):
            row = work[k : k + 1, :]
            column = work[:, k : k + 1]
            inverse = 1.0 / work[k : k + 1, k : k + 1]
            scaled = jnp.where(lane[:1] == k, -inverse, row * inverse)
            works[i] = jnp.where(lane == k, 0.0, work) - column * scaled
    return [work[size:] for work in works]


def update_kernel(*refs):
    *gram_refs, solution_ref, resid_ref, dirs_ref, image_ref, next_solution_ref, next_resid_ref, next_dirs_ref = refs
    grams = sum((ref[...] for ref in gram_refs[1:]), gram_refs[0][...])
    rhs = grams.shape[0]
    rr, rq, _, dq, qr, qq = (grams[:, i * rhs : (i + 1) * rhs] for i in range(6))
    old = 0.5 * (rr + rr.T)
    curvature = 0.5 * (dq + dq.T)
    rows = lax.broadcasted_iota(jnp.int32, (rhs, rhs), 0)
    cols = lax.broadcasted_iota(jnp.int32, (rhs, rhs), 1)
    unit = jnp.where(rows == cols, 1.0, 0.0).astype(jnp.float32)
    alpha_t, old_inverse = right_divide((curvature, old), (old, unit))
    new = rr - dot_nn(alpha_t, qr) + dot_nt(dot_nn(alpha_t, qq) - rq, alpha_t)
    beta_t = dot_nn(new, old_inverse)
    dirs = dirs_ref[...]
    next_resid = resid_ref[...] - dot_nn(alpha_t, image_ref[...])
    next_resid_ref[...] = next_resid
    next_solution_ref[...] = solution_ref[...] + dot_nn(alpha_t, dirs)
    next_dirs_ref[...] = next_resid + dot_nn(beta_t, dirs)


def exchanged(value, axis, stride):
    return lax.ppermute(value, axis, [(i, i ^ stride) for i in range(lax.axis_size(axis))])


def rounds(count):
    bits = [1 << i for i in range((count - 1).bit_length())]
    groups = [bits[:1]] + [bits[i : i + 2] for i in range(1, len(bits), 2)] if len(bits) % 2 else [bits[i : i + 2] for i in range(0, len(bits), 2)]
    return [[group[0]] if len(group) == 1 else [group[0], group[1], group[0] + group[1]] for group in groups]


def gathered(block, index, strides, slab):
    parts = [block] + [exchanged(block, "row", stride) for stride in strides]
    count = len(parts)
    shift = strides[0].bit_length() - 1
    slots = jnp.stack([((index ^ stride) >> shift) & (count - 1) for stride in (0, *strides)])
    return pl.pallas_call(
        place_kernel,
        in_specs=[SMEM, HBM] + [VMEM] * count,
        out_specs=VMEM,
        out_shape=jax.ShapeDtypeStruct((block.shape[0], count * block.shape[1]), block.dtype),
        compiler_params=pltpu.CompilerParams(vmem_limit_bytes=2 << 20),
        name="place",
    )(slots, slab, *parts)


def local(solution, residual, direction, normal, weights):
    rhs, count = direction.shape[1:]
    dirs, resid = direction[0], residual[0]
    slab = pltpu.with_memory_space_constraint(normal[0], pltpu.HBM)
    low_type = jax.ShapeDtypeStruct((rhs, count), jnp.bfloat16)
    own_low = pl.pallas_call(
        round_kernel,
        in_specs=[VMEM],
        out_specs=VMEM,
        out_shape=low_type,
        compiler_params=pltpu.CompilerParams(vmem_limit_bytes=2 << 20),
        name="low",
    )(dirs)
    row = lax.axis_index("row")
    *near, far = rounds(lax.axis_size("row"))
    block = own_low
    for strides in near:
        block = gathered(block, row, strides, slab)
    width = block.shape[1]
    blocks = [exchanged(block, "row", stride) for stride in far]
    shift = far[0].bit_length() - 1
    places = [row >> shift] + [(row ^ stride) >> shift for stride in far]
    months = lax.axis_size("tm")
    month = lax.axis_index("tm")

    wide = jax.ShapeDtypeStruct((rhs, count), jnp.float32)
    params = pltpu.CompilerParams(vmem_limit_bytes=8 << 20)
    product, own_low = pl.pallas_call(
        first_kernel,
        in_specs=[SMEM] + [VMEM] * 4,
        out_specs=[VMEM] * 2,
        out_shape=[wide, low_type],
        compiler_params=params,
        cost_estimate=pl.CostEstimate(flops=2 * rhs * count * width, bytes_accessed=2 * count * width, transcendentals=0),
        name="first",
    )(jnp.stack(places[:2]), block, blocks[0], own_low, normal[0])
    before = lax.ppermute(own_low, "tm", [(i, i + 1) for i in range(months - 1)])
    after = lax.ppermute(own_low, "tm", [(i + 1, i) for i in range(months - 1)])
    late = blocks[1:]
    image, grams = pl.pallas_call(
        functools.partial(image_kernel, len(late)),
        in_specs=[SMEM] * 2 + [VMEM] * (len(late) + 7),
        out_specs=[VMEM] * 2,
        out_shape=[wide, jax.ShapeDtypeStruct((rhs, 6 * rhs), jnp.float32)],
        compiler_params=params,
        name="image",
    )(
        jnp.stack(places[2:]), jnp.stack([month > 0, month < months - 1]).astype(jnp.int32),
        *late, normal[0], product, dirs, resid, before, after, weights[None],
    )
    steps = [(axis, strides) for axis in ("row", "tm") for strides in rounds(lax.axis_size(axis))]
    parts = [grams]
    for axis, strides in steps:
        total = functools.reduce(jnp.add, parts)
        parts = [total] + [exchanged(total, axis, stride) for stride in strides]
    outs = pl.pallas_call(
        update_kernel,
        in_specs=[VMEM] * (len(parts) + 4),
        out_specs=[VMEM] * 3,
        out_shape=[wide] * 3,
        compiler_params=params,
        name="update",
    )(*parts, solution[0], resid, dirs, image)
    return tuple(out[None] for out in outs)


def solution(mesh):
    placed = (
        P("tm", None, "row"),
        P("tm", None, "row"),
        P("tm", None, "row"),
        P("tm", "row", None),
        P("row"),
    )
    return jax.shard_map(
        local,
        mesh=mesh,
        in_specs=placed,
        out_specs=(P("tm", None, "row"), P("tm", None, "row"), P("tm", None, "row")),
        check_vma=False,
    )
```

time: 122 us -> 43 us (0.35)
  blocking collectives: 91.2 us -> 0 us
  matrix products: 14.4 us -> 0 us
  starting transfers between devices: 6.21 us -> 19.8 us
  waiting for transfers between devices: 0.01 us -> 11.3 us
  Pallas kernels: 0 us -> 9.84 us
  other arithmetic: 8.94 us -> 0.31 us
    psum x2 -> x0, blocking collectives: 81.9 us -> none  [the longest x1 41.1 us: local(): gram_new = lax.psum(local_gram(next_resid, next_resid), ('tm', 'row'))]
    dot_general x7 -> x0, matrix products: 13.7 us -> none  [the longest x1 10.2 us: local(): lax.dot_general(lax.all_gather(own_low, 'row', axis=1, tiled=True), slab,...]
    ppermute x2 -> x13, starting transfers between devices: 6.21 us -> 19.8 us  [the longest x11 13.9 us: exchanged(): lax.ppermute(value, axis, [(i, i ^ stride) for i in range(lax.axis_size(a...]
    ppermute x2 -> x13, waiting for transfers between devices: 0.01 us -> 11.3 us  [the longest x11 9.81 us: exchanged(): lax.ppermute(value, axis, [(i, i ^ stride) for i in range(lax.axis_size(a...]
    pallas_call x0 -> x5, Pallas kernels: none -> 9.84 us  [the longest x1 3.26 us: local(): pl.pallas_call(update_kernel, in_specs=[VMEM] * (len(parts) + 4), out_spe...]
    all_gather x1 -> x0, blocking collectives: 9.34 us -> none  [local(): lax.all_gather(own_low, 'row', axis=1, tiled=True)]
    another operation x10 -> x3, other arithmetic: 8.03 us -> 0.22 us  [the longest x1 0.07 us: local(): jnp.stack(places[2:])]
  transfers between devices with their start and end apart: 2 -> 13, of which waited for: 0 -> 9; matrix products, arithmetic and copies ran while one was open for 1% -> 1% of each run, Pallas kernels for 0% -> 7%
where the time goes in v1:
time: 43 us; the launch traced here: 42.8 us
  starting transfers between devices  19.8 us (46%)
  waiting for transfers between devices  11.3 us (26%)
  Pallas kernels  9.84 us (23%)
  local copies, waits for them, and re-layouts  0.85 us (2%)
  between operations  0.69 us (2%)
    ppermute x11, starting transfers between devices, exchanged(): lax.ppermute(value, axis, [(i, i ^ stride) for i in range(lax.axis_size(a...  13.9 us
    ppermute x11, waiting for transfers between devices, exchanged(): lax.ppermute(value, axis, [(i, i ^ stride) for i in range(lax.axis_size(a...  9.81 us
    ppermute x1, starting transfers between devices, local(): lax.ppermute(own_low, 'tm', [(i, i + 1) for i in range(months - 1)])  4.55 us
    pallas_call x1, Pallas kernels, local(): pl.pallas_call(update_kernel, in_specs=[VMEM] * (len(parts) + 4), out_spe...  3.26 us
    pallas_call x1, Pallas kernels, local(): pl.pallas_call(functools.partial(image_kernel, len(late)), in_specs=[SMEM...  3.21 us
    pallas_call x1, Pallas kernels, local(): pl.pallas_call(first_kernel, in_specs=[SMEM] + [VMEM] * 4, out_specs=[VME...  2.81 us
    ppermute x1, waiting for transfers between devices, local(): lax.ppermute(own_low, 'tm', [(i, i + 1) for i in range(months - 1)])  1.49 us
    ppermute x1, starting transfers between devices, local(): after = lax.ppermute(own_low, 'tm', [(i + 1, i) for i in range(months - 1)])  1.3 us
  transfers between devices with their start and end apart: 13, of which 9 were waited for; matrix products, arithmetic and copies ran while one was open for 1% of the time, Pallas kernels for 7%

profile of v1, /device:TPU:0, one launch (start us, length us, event | category | flops | bytes accessed | tf_op | source)
XLA Modules:
  0.0 42.8 jit_solution(16458428053815944886)
XLA Ops:
  0.6 0.0 copy-start.1
  0.6 0.8 %copy-done.1 = f32[1,16,1024]{2,1,0:T(8,128)S(1)} copy-done((f32[1,16,1024]{2,1,0:T(8,128)S(1)}, f32[1,16,1024]{2,1,0:T(8,128)}, u32[]{:S(2)}) %copy-start.1) | copy-done | bytes 65560
  1.5 0.5 %collective-permute-start = (bf16[16,1024]{1,0:T(8,128)(2,1)S(1)}, bf16[16,1024]{1,0:T(8,128)(2,1)S(1)}, u32[]{:S(2)}, u32[]{:S(2)}) collective-permute-start(bf16[16,1024]{1,0:T(8,128)(2,1)S(1)} %low.1.refs_0_.low_ref), channel_id=1, source_target_pairs={{0,1},{1,0},{2,3},{3,2},{4,5},{5,4},{6,7},{7,6},{8,9},{9,8},{10,11... | collective-permute-start | bytes 98312 | tf_op jit(solution)/shard_map/ppermute | solution.py:115
  1.9 0.1 pad_add_fusion.places_ref
  2.0 0.1 pad_add_fusion.1.slots_ref
  2.1 0.0 copy-start
  2.1 0.7 %collective-permute-done.refs_1_ = bf16[16,1024]{1,0:T(8,128)(2,1)S(1)} collective-permute-done((bf16[16,1024]{1,0:T(8,128)(2,1)S(1)}, bf16[16,1024]{1,0:T(8,128)(2,1)S(1)}, u32[]{:S(2)}, u32[]{:S(2)}) %collective-permute-start) | collective-permute-done | bytes 32800 | tf_op jit(solution)/shard_map/ppermute | solution.py:115
  2.8 0.0 copy-start.2
  2.8 0.0 copy-start.3
  2.8 0.0 copy-start.5
  2.8 0.5 %place.1.block_ref = bf16[16,2048]{1,0:T(8,128)(2,1)S(1)} custom-call(s32[2]{0:T(128)S(1)} %pad_add_fusion.1.slots_ref, bf16[1024,8192]{1,0:T(8,128)(2,1)} %bitcast.16, bf16[16,1024]{1,0:T(8,128)(2,1)S(1)} %low.1.refs_0_.low_ref, bf16[16,1024]{1,0:T(8,128)(2,1)S(1)} %collective-permute-done.refs_1_), custom_call_target="tpu_custom_call" | custom-call | tf_op jit(solution)/shard_map/place/pallas_call | solution.py:129
  3.4 2.9 %collective-permute-start.3 = (bf16[16,2048]{1,0:T(8,128)(2,1)S(1)}, bf16[16,2048]{1,0:T(8,128)(2,1)S(1)}, u32[]{:S(2)}, u32[]{:S(2)}) collective-permute-start(bf16[16,2048]{1,0:T(8,128)(2,1)S(1)} %place.1.block_ref), channel_id=1, source_target_pairs={{0,2},{1,3},{2,0},{3,1},{4,6},{5,7},{6,4},{7,5},{8,10},{9,11},{10,... | collective-permute-start | bytes 196616 | tf_op jit(solution)/shard_map/ppermute | solution.py:115
  6.3 0.1 pad_add_fusion.2.places_ref
  6.3 0.0 copy-start.4
  6.3 1.5 %collective-permute-start.2 = (bf16[16,2048]{1,0:T(8,128)(2,1)S(1)}, bf16[16,2048]{1,0:T(8,128)(2,1)S(1)}, u32[]{:S(2)}, u32[]{:S(2)}) collective-permute-start(bf16[16,2048]{1,0:T(8,128)(2,1)S(1)} %place.1.block_ref), channel_id=1, source_target_pairs={{0,6},{1,7},{2,4},{3,5},{4,2},{5,3},{6,0},{7,1},{8,14},{9,15},{10,... | collective-permute-start | bytes 196616 | tf_op jit(solution)/shard_map/ppermute | solution.py:115
  7.8 0.1 collective-permute-start.1
  7.9 0.7 %collective-permute-done.3.next_ref = bf16[16,2048]{1,0:T(8,128)(2,1)S(1)} collective-permute-done((bf16[16,2048]{1,0:T(8,128)(2,1)S(1)}, bf16[16,2048]{1,0:T(8,128)(2,1)S(1)}, u32[]{:S(2)}, u32[]{:S(2)}) %collective-permute-start.3) | collective-permute-done | bytes 65568 | tf_op jit(solution)/shard_map/ppermute | solution.py:115
  8.7 0.0 copy-done
  8.7 2.8 %first.1 = (f32[16,1024]{1,0:T(8,128)S(1)}, bf16[16,1024]{1,0:T(8,128)(2,1)S(1)}) custom-call(s32[2]{0:T(128)S(1)} %pad_add_fusion.2.places_ref, bf16[16,2048]{1,0:T(8,128)(2,1)S(1)} %place.1.block_ref, bf16[16,2048]{1,0:T(8,128)(2,1)S(1)} %collective-permute-done.3.next_ref, bf16[16,1024]{1,0:T(8,128)(2,1)S(1)} %low.1.refs_0_.low_ref, ...), custom_call_target="tpu_custom_call" | custom-call | flops 67108864 | bytes 4194304 | tf_op jit(solution)/shard_map/first/pallas_call | solution.py:166
  11.5 1.3 %collective-permute-start.5 = (bf16[16,1024]{1,0:T(8,128)(2,1)S(1)}, bf16[16,1024]{1,0:T(8,128)(2,1)S(1)}, u32[]{:S(2)}, u32[]{:S(2)}) collective-permute-start(bf16[16,1024]{1,0:T(8,128)(2,1)S(1)} %get-tuple-element.11), channel_id=1, source_target_pairs={{8,0},{16,8},{24,16},{9,1},{17,9},{25,17},{10,2},{18,10},{26,18},{... | collective-permute-start | bytes 98312 | tf_op jit(solution)/shard_map/ppermute | solution.py:176
  12.8 4.5 %collective-permute-start.4 = (bf16[16,1024]{1,0:T(8,128)(2,1)S(1)}, bf16[16,1024]{1,0:T(8,128)(2,1)S(1)}, u32[]{:S(2)}, u32[]{:S(2)}) collective-permute-start(bf16[16,1024]{1,0:T(8,128)(2,1)S(1)} %get-tuple-element.11), channel_id=1, source_target_pairs={{0,8},{8,16},{16,24},{1,9},{9,17},{17,25},{2,10},{10,18},{18,26},{... | collective-permute-start | bytes 98312 | tf_op jit(solution)/shard_map/ppermute | solution.py:175
  17.3 0.1 add_convert_fusion.ends_ref
  17.4 0.0 collective-permute-done.2.refs_1_
  17.4 0.0 collective-permute-done.1.refs_0_
  17.4 0.0 collective-permute-done.5.refs_7_
  17.4 1.5 %collective-permute-done.4.refs_6_ = bf16[16,1024]{1,0:T(8,128)(2,1)S(1)} collective-permute-done((bf16[16,1024]{1,0:T(8,128)(2,1)S(1)}, bf16[16,1024]{1,0:T(8,128)(2,1)S(1)}, u32[]{:S(2)}, u32[]{:S(2)}) %collective-permute-start.4) | collective-permute-done | bytes 32800 | tf_op jit(solution)/shard_map/ppermute | solution.py:175
  18.9 0.0 copy-done.2
  18.9 0.0 copy-done.3
  18.9 0.0 copy-done.5
  18.9 3.2 %image.1 = (f32[16,1024]{1,0:T(8,128)S(1)}, f32[16,96]{1,0:T(8,128)S(1)}) custom-call(s32[2]{0:T(128)S(1)} %pad_add_fusion.places_ref, s32[2]{0:T(128)S(1)} %add_convert_fusion.ends_ref, bf16[16,2048]{1,0:T(8,128)(2,1)S(1)} %collective-permute-done.1.refs_0_, bf16[16,2048]{1,0:T(8,128)(2,1)S(1)} %collective-permute-done.2.refs_1_, ...), custom_call_target="tpu_custom_call" | custom-call | tf_op jit(solution)/shard_map/image/pallas_call | solution.py:178
  22.1 0.0 collective-permute-start.6
  22.2 1.2 %collective-permute-done.6 = f32[16,96]{1,0:T(8,128)S(1)} collective-permute-done((f32[16,96]{1,0:T(8,128)S(1)}, f32[16,96]{1,0:T(8,128)S(1)}, u32[]{:S(2)}, u32[]{:S(2)}) %collective-permute-start.6) | collective-permute-done | bytes 6176 | tf_op jit(solution)/shard_map/ppermute | solution.py:115
  23.3 3.4 %collective-permute-start.9 = (f32[16,96]{1,0:T(8,128)S(1)}, f32[16,96]{1,0:T(8,128)S(1)}, u32[]{:S(2)}, u32[]{:S(2)}) collective-permute-start(f32[16,96]{1,0:T(8,128)S(1)} %add.12), channel_id=1, source_target_pairs={{0,6},{1,7},{2,4},{3,5},{4,2},{5,3},{6,0},{7,1},{8,14},{9,15},{10,... | collective-permute-start | bytes 18440 | tf_op jit(solution)/shard_map/ppermute | solution.py:115
  26.7 0.2 collective-permute-start.8
  26.9 0.4 collective-permute-start.7
  27.3 1.1 %collective-permute-done.9 = f32[16,96]{1,0:T(8,128)S(1)} collective-permute-done((f32[16,96]{1,0:T(8,128)S(1)}, f32[16,96]{1,0:T(8,128)S(1)}, u32[]{:S(2)}, u32[]{:S(2)}) %collective-permute-start.9) | collective-permute-done | bytes 6176 | tf_op jit(solution)/shard_map/ppermute | solution.py:115
  28.4 2.0 %collective-permute-done.8 = f32[16,96]{1,0:T(8,128)S(1)} collective-permute-done((f32[16,96]{1,0:T(8,128)S(1)}, f32[16,96]{1,0:T(8,128)S(1)}, u32[]{:S(2)}, u32[]{:S(2)}) %collective-permute-start.8) | collective-permute-done | bytes 6176 | tf_op jit(solution)/shard_map/ppermute | solution.py:115
  30.4 0.2 collective-permute-done.7
  30.6 4.3 %collective-permute-start.12 = (f32[16,96]{1,0:T(8,128)S(1)}, f32[16,96]{1,0:T(8,128)S(1)}, u32[]{:S(2)}, u32[]{:S(2)}) collective-permute-start(f32[16,96]{1,0:T(8,128)S(1)} %add_add_fusion.refs_0_), channel_id=1, source_target_pairs={{0,24},{8,16},{16,8},{24,0},{1,25},{9,17},{17,9},{25,1},{2,26},{10... | collective-permute-start | bytes 18440 | tf_op jit(solution)/shard_map/ppermute | solution.py:115
  34.9 0.0 collective-permute-start.11
  34.9 0.6 %collective-permute-start.10 = (f32[16,96]{1,0:T(8,128)S(1)}, f32[16,96]{1,0:T(8,128)S(1)}, u32[]{:S(2)}, u32[]{:S(2)}) collective-permute-start(f32[16,96]{1,0:T(8,128)S(1)} %add_add_fusion.refs_0_), channel_id=1, source_target_pairs={{0,8},{8,0},{16,24},{24,16},{1,9},{9,1},{17,25},{25,17},{2,10},{10... | collective-permute-start | bytes 18440 | tf_op jit(solution)/shard_map/ppermute | solution.py:115
  35.6 1.0 %collective-permute-done.12.refs_3_ = f32[16,96]{1,0:T(8,128)S(1)} collective-permute-done((f32[16,96]{1,0:T(8,128)S(1)}, f32[16,96]{1,0:T(8,128)S(1)}, u32[]{:S(2)}, u32[]{:S(2)}) %collective-permute-start.12) | collective-permute-done | bytes 6176 | tf_op jit(solution)/shard_map/ppermute | solution.py:115
  36.6 2.9 %collective-permute-done.11.refs_2_ = f32[16,96]{1,0:T(8,128)S(1)} collective-permute-done((f32[16,96]{1,0:T(8,128)S(1)}, f32[16,96]{1,0:T(8,128)S(1)}, u32[]{:S(2)}, u32[]{:S(2)}) %collective-permute-start.11) | collective-permute-done | bytes 6176 | tf_op jit(solution)/shard_map/ppermute | solution.py:115
  39.5 0.0 collective-permute-done.10.refs_1_
  39.5 0.0 copy-done.4
  39.5 3.3 %update.1 = (f32[16,1024]{1,0:T(8,128)}, f32[16,1024]{1,0:T(8,128)}, f32[16,1024]{1,0:T(8,128)}) custom-call(f32[16,96]{1,0:T(8,128)S(1)} %add_add_fusion.refs_0_, f32[16,96]{1,0:T(8,128)S(1)} %collective-permute-done.10.refs_1_, f32[16,96]{1,0:T(8,128)S(1)} %collective-permute-done.11.refs_2_, f32[16,96]{1,0:T(8,128)S(1)} %collective-permute-done.12.refs_3_, ...), custom_call_target="tpu_custom_call" | custom-call | tf_op jit(solution)/shard_map/update/pallas_call | solution.py:194
  (3 shorter events, 0.0 us)
Async XLA Ops:
  0.6 0.8 %copy-start.1 = (f32[1,16,1024]{2,1,0:T(8,128)S(1)}, f32[1,16,1024]{2,1,0:T(8,128)}, u32[]{:S(2)}) copy-start(f32[1,16,1024]{2,1,0:T(8,128)} %param.7) | copy-start | bytes 196612
  1.5 1.3 %collective-permute-start = (bf16[16,1024]{1,0:T(8,128)(2,1)S(1)}, bf16[16,1024]{1,0:T(8,128)(2,1)S(1)}, u32[]{:S(2)}, u32[]{:S(2)}) collective-permute-start(bf16[16,1024]{1,0:T(8,128)(2,1)S(1)} %low.1.refs_0_.low_ref), channel_id=1, source_target_pairs={{0,1},{1,0},{2,3},{3,2},{4,5},{5,4},{6,7},{7,6},{8,9},{9,8},{10,11... | collective-permute-start | bytes 98312 | tf_op jit(solution)/shard_map/ppermute | solution.py:115
  2.1 6.6 %copy-start = (bf16[1,1024,8192]{2,1,0:T(8,128)(2,1)S(1)}, bf16[1,1024,8192]{2,1,0:T(8,128)(2,1)}, u32[]{:S(2)}) copy-start(bf16[1,1024,8192]{2,1,0:T(8,128)(2,1)} %param.8) | copy-start | bytes 50331652
  2.8 16.1 %copy-start.2 = (f32[1,16,1024]{2,1,0:T(8,128)S(1)}, f32[1,16,1024]{2,1,0:T(8,128)}, u32[]{:S(2)}) copy-start(f32[1,16,1024]{2,1,0:T(8,128)} %param.7) | copy-start | bytes 196612
  2.8 16.1 %copy-start.3 = (f32[1,16,1024]{2,1,0:T(8,128)S(1)}, f32[1,16,1024]{2,1,0:T(8,128)}, u32[]{:S(2)}) copy-start(f32[1,16,1024]{2,1,0:T(8,128)} %param.6) | copy-start | bytes 196612
  2.8 16.1 %copy-start.5 = (f32[1024]{0:T(1024)S(1)}, f32[1024]{0:T(1024)}, u32[]{:S(2)}) copy-start(f32[1024]{0:T(1024)} %param.9) | copy-start | bytes 12292
  3.4 5.3 %collective-permute-start.3 = (bf16[16,2048]{1,0:T(8,128)(2,1)S(1)}, bf16[16,2048]{1,0:T(8,128)(2,1)S(1)}, u32[]{:S(2)}, u32[]{:S(2)}) collective-permute-start(bf16[16,2048]{1,0:T(8,128)(2,1)S(1)} %place.1.block_ref), channel_id=1, source_target_pairs={{0,2},{1,3},{2,0},{3,1},{4,6},{5,7},{6,4},{7,5},{8,10},{9,11},{10,... | collective-permute-start | bytes 196616 | tf_op jit(solution)/shard_map/ppermute | solution.py:115
  6.3 33.2 %copy-start.4 = (f32[1,16,1024]{2,1,0:T(8,128)S(1)}, f32[1,16,1024]{2,1,0:T(8,128)}, u32[]{:S(2)}) copy-start(f32[1,16,1024]{2,1,0:T(8,128)} %param.5) | copy-start | bytes 196612
  6.3 11.1 %collective-permute-start.2 = (bf16[16,2048]{1,0:T(8,128)(2,1)S(1)}, bf16[16,2048]{1,0:T(8,128)(2,1)S(1)}, u32[]{:S(2)}, u32[]{:S(2)}) collective-permute-start(bf16[16,2048]{1,0:T(8,128)(2,1)S(1)} %place.1.block_ref), channel_id=1, source_target_pairs={{0,6},{1,7},{2,4},{3,5},{4,2},{5,3},{6,0},{7,1},{8,14},{9,15},{10,... | collective-permute-start | bytes 196616 | tf_op jit(solution)/shard_map/ppermute | solution.py:115
  7.8 9.6 %collective-permute-start.1 = (bf16[16,2048]{1,0:T(8,128)(2,1)S(1)}, bf16[16,2048]{1,0:T(8,128)(2,1)S(1)}, u32[]{:S(2)}, u32[]{:S(2)}) collective-permute-start(bf16[16,2048]{1,0:T(8,128)(2,1)S(1)} %place.1.block_ref), channel_id=1, source_target_pairs={{0,4},{1,5},{2,6},{3,7},{4,0},{5,1},{6,2},{7,3},{8,12},{9,13},{10,... | collective-permute-start | bytes 196616 | tf_op jit(solution)/shard_map/ppermute | solution.py:115
  11.5 5.9 %collective-permute-start.5 = (bf16[16,1024]{1,0:T(8,128)(2,1)S(1)}, bf16[16,1024]{1,0:T(8,128)(2,1)S(1)}, u32[]{:S(2)}, u32[]{:S(2)}) collective-permute-start(bf16[16,1024]{1,0:T(8,128)(2,1)S(1)} %get-tuple-element.11), channel_id=1, source_target_pairs={{8,0},{16,8},{24,16},{9,1},{17,9},{25,17},{10,2},{18,10},{26,18},{... | collective-permute-start | bytes 98312 | tf_op jit(solution)/shard_map/ppermute | solution.py:176
  12.8 6.1 %collective-permute-start.4 = (bf16[16,1024]{1,0:T(8,128)(2,1)S(1)}, bf16[16,1024]{1,0:T(8,128)(2,1)S(1)}, u32[]{:S(2)}, u32[]{:S(2)}) collective-permute-start(bf16[16,1024]{1,0:T(8,128)(2,1)S(1)} %get-tuple-element.11), channel_id=1, source_target_pairs={{0,8},{8,16},{16,24},{1,9},{9,17},{17,25},{2,10},{10,18},{18,26},{... | collective-permute-start | bytes 98312 | tf_op jit(solution)/shard_map/ppermute | solution.py:175
  22.1 1.2 %collective-permute-start.6 = (f32[16,96]{1,0:T(8,128)S(1)}, f32[16,96]{1,0:T(8,128)S(1)}, u32[]{:S(2)}, u32[]{:S(2)}) collective-permute-start(f32[16,96]{1,0:T(8,128)S(1)} %get-tuple-element.12), channel_id=1, source_target_pairs={{0,1},{1,0},{2,3},{3,2},{4,5},{5,4},{6,7},{7,6},{8,9},{9,8},{10,11... | collective-permute-start | bytes 18440 | tf_op jit(solution)/shard_map/ppermute | solution.py:115
  23.3 5.0 %collective-permute-start.9 = (f32[16,96]{1,0:T(8,128)S(1)}, f32[16,96]{1,0:T(8,128)S(1)}, u32[]{:S(2)}, u32[]{:S(2)}) collective-permute-start(f32[16,96]{1,0:T(8,128)S(1)} %add.12), channel_id=1, source_target_pairs={{0,6},{1,7},{2,4},{3,5},{4,2},{5,3},{6,0},{7,1},{8,14},{9,15},{10,... | collective-permute-start | bytes 18440 | tf_op jit(solution)/shard_map/ppermute | solution.py:115
  26.7 3.7 %collective-permute-start.8 = (f32[16,96]{1,0:T(8,128)S(1)}, f32[16,96]{1,0:T(8,128)S(1)}, u32[]{:S(2)}, u32[]{:S(2)}) collective-permute-start(f32[16,96]{1,0:T(8,128)S(1)} %add.12), channel_id=1, source_target_pairs={{0,4},{1,5},{2,6},{3,7},{4,0},{5,1},{6,2},{7,3},{8,12},{9,13},{10,... | collective-permute-start | bytes 18440 | tf_op jit(solution)/shard_map/ppermute | solution.py:115
  26.9 3.7 %collective-permute-start.7 = (f32[16,96]{1,0:T(8,128)S(1)}, f32[16,96]{1,0:T(8,128)S(1)}, u32[]{:S(2)}, u32[]{:S(2)}) collective-permute-start(f32[16,96]{1,0:T(8,128)S(1)} %add.12), channel_id=1, source_target_pairs={{0,2},{1,3},{2,0},{3,1},{4,6},{5,7},{6,4},{7,5},{8,10},{9,11},{10,... | collective-permute-start | bytes 18440 | tf_op jit(solution)/shard_map/ppermute | solution.py:115
  30.6 6.0 %collective-permute-start.12 = (f32[16,96]{1,0:T(8,128)S(1)}, f32[16,96]{1,0:T(8,128)S(1)}, u32[]{:S(2)}, u32[]{:S(2)}) collective-permute-start(f32[16,96]{1,0:T(8,128)S(1)} %add_add_fusion.refs_0_), channel_id=1, source_target_pairs={{0,24},{8,16},{16,8},{24,0},{1,25},{9,17},{17,9},{25,1},{2,26},{10... | collective-permute-start | bytes 18440 | tf_op jit(solution)/shard_map/ppermute | solution.py:115
  34.9 4.5 %collective-permute-start.11 = (f32[16,96]{1,0:T(8,128)S(1)}, f32[16,96]{1,0:T(8,128)S(1)}, u32[]{:S(2)}, u32[]{:S(2)}) collective-permute-start(f32[16,96]{1,0:T(8,128)S(1)} %add_add_fusion.refs_0_), channel_id=1, source_target_pairs={{0,16},{8,24},{16,0},{24,8},{1,17},{9,25},{17,1},{25,9},{2,18},{10... | collective-permute-start | bytes 18440 | tf_op jit(solution)/shard_map/ppermute | solution.py:115
  34.9 4.5 %collective-permute-start.10 = (f32[16,96]{1,0:T(8,128)S(1)}, f32[16,96]{1,0:T(8,128)S(1)}, u32[]{:S(2)}, u32[]{:S(2)}) collective-permute-start(f32[16,96]{1,0:T(8,128)S(1)} %add_add_fusion.refs_0_), channel_id=1, source_target_pairs={{0,8},{8,0},{16,24},{24,16},{1,9},{9,1},{17,25},{25,17},{2,10},{10... | collective-permute-start | bytes 18440 | tf_op jit(solution)/shard_map/ppermute | solution.py:115

commit v2 on v1

--- a/solution.py
+++ b/solution.py
@@ -23,18 +23,18 @@
     return jnp.dot(left, right, precision=HIGH, preferred_element_type=jnp.float32)
 
 
-def round_kernel(wide_ref, low_ref):
-    low_ref[...] = wide_ref[...].astype(jnp.bfloat16)
-
-
-def place_kernel(slots_ref, _, *refs):
-    *parts, out_ref = refs
+def rounded(ref):
+    return ref[...].astype(jnp.bfloat16).astype(jnp.float32)
+
+
+def place_kernel(count, *refs):
+    slots, parts, out_ref = refs[:count], refs[count + 1 : 2 * count + 1], refs[-1]
     width = parts[0].shape[1]
-    for i, part in enumerate(parts):
-        out_ref[:, pl.ds(pl.multiple_of(slots_ref[i] * width, width), width)] = part[...]
-
-
-def product_of(places_ref, blocks, slab_ref, sum_ref, out_ref):
+    for slot, part in zip(slots, parts, strict=True):
+        out_ref[:, pl.ds(pl.multiple_of(slot[0] * width, width), width)] = part[...].astype(out_ref.dtype)
+
+
+def product_of(places, blocks, slab_ref, sum_ref, out_ref):
     rows = slab_ref.shape[0]
     width = blocks[0].shape[1]
     tile = min(TILE, rows)
@@ -42,7 +42,7 @@
         part = pl.ds(start, tile)
         total = None if sum_ref is None else sum_ref[:, part]
         for i, block in enumerate(blocks):
-            columns = pl.ds(pl.multiple_of(places_ref[i] * width, width), width)
+            columns = pl.ds(pl.multiple_of(places[i][0] * width, width), width)
             term = lax.dot_general(
                 block[...], slab_ref[part, columns], ROWS_BY_ROWS, preferred_element_type=jnp.float32
             )
@@ -50,25 +50,22 @@
         out_ref[:, part] = total
 
 
-def first_kernel(places_ref, block_ref, next_ref, low_ref, slab_ref, out_ref, low_out_ref):
-    low_out_ref[...] = low_ref[...]
-    product_of(places_ref, [block_ref, next_ref], slab_ref, None, out_ref)
-
-
-def image_kernel(count, places_ref, ends_ref, *refs):
-    blocks, refs = refs[:count], refs[count:]
-    slab_ref, sum_ref, dirs_ref, resid_ref, before_ref, after_ref, weights_ref = refs[:7]
-    image_ref, grams_ref = refs[7:]
+def first_kernel(place_ref, next_place_ref, block_ref, next_ref, slab_ref, _, out_ref):
+    product_of([place_ref, next_place_ref], [block_ref, next_ref], slab_ref, None, out_ref)
+
+
+def image_kernel(count, *refs):
+    places, blocks, refs = refs[:count], refs[count : 2 * count], refs[2 * count :]
+    has_before_ref, has_after_ref, slab_ref, sum_ref, dirs_ref, resid_ref, before_ref, after_ref, weights_ref = refs[:9]
+    image_ref, grams_ref = refs[9:]
     dirs = dirs_ref[...]
     resid = resid_ref[...]
-    centre = dirs.astype(jnp.bfloat16).astype(jnp.float32)
-    has_prev = ends_ref[0].astype(jnp.float32)
-    has_next = ends_ref[1].astype(jnp.float32)
-    coupled = has_prev * (centre - before_ref[...].astype(jnp.float32)) + has_next * (
-        centre - after_ref[...].astype(jnp.float32)
-    )
+    centre = rounded(dirs_ref)
+    has_before = has_before_ref[0].astype(jnp.float32)
+    has_after = has_after_ref[0].astype(jnp.float32)
+    coupled = has_before * (centre - rounded(before_ref)) + has_after * (centre - rounded(after_ref))
     image_ref[...] = sum_ref[...] + weights_ref[...] * coupled
-    product_of(places_ref, blocks, slab_ref, image_ref, image_ref)
+    product_of(places, blocks, slab_ref, image_ref, image_ref)
     image = image_ref[...]
     left = jnp.concatenate([resid, dirs, image], axis=0)
     right = jnp.concatenate([resid, image], axis=0)
@@ -121,70 +118,67 @@
     return [[group[0]] if len(group) == 1 else [group[0], group[1], group[0] + group[1]] for group in groups]
 
 
+def scalar(value):
+    return jnp.asarray(value, jnp.int32).reshape(1)
+
+
 def gathered(block, index, strides, slab):
     parts = [block] + [exchanged(block, "row", stride) for stride in strides]
     count = len(parts)
     shift = strides[0].bit_length() - 1
-    slots = jnp.stack([((index ^ stride) >> shift) & (count - 1) for stride in (0, *strides)])
+    slots = [scalar(((index ^ stride) >> shift) & (count - 1)) for stride in (0, *strides)]
     return pl.pallas_call(
-        place_kernel,
-        in_specs=[SMEM, HBM] + [VMEM] * count,
+        functools.partial(place_kernel, count),
+        in_specs=[SMEM] * count + [HBM] + [VMEM] * count,
         out_specs=VMEM,
-        out_shape=jax.ShapeDtypeStruct((block.shape[0], count * block.shape[1]), block.dtype),
+        out_shape=jax.ShapeDtypeStruct((block.shape[0], count * block.shape[1]), jnp.bfloat16),
         compiler_params=pltpu.CompilerParams(vmem_limit_bytes=2 << 20),
         name="place",
-    )(slots, slab, *parts)
+    )(*slots, slab, *parts)
 
 
 def local(solution, residual, direction, normal, weights):
     rhs, count = direction.shape[1:]
     dirs, resid = direction[0], residual[0]
     slab = pltpu.with_memory_space_constraint(normal[0], pltpu.HBM)
-    low_type = jax.ShapeDtypeStruct((rhs, count), jnp.bfloat16)
-    own_low = pl.pallas_call(
-        round_kernel,
-        in_specs=[VMEM],
-        out_specs=VMEM,
-        out_shape=low_type,
-        compiler_params=pltpu.CompilerParams(vmem_limit_bytes=2 << 20),
-        name="low",
-    )(dirs)
     row = lax.axis_index("row")
     *near, far = rounds(lax.axis_size("row"))
-    block = own_low
+    block = dirs
     for strides in near:
         block = gathered(block, row, strides, slab)
     width = block.shape[1]
     blocks = [exchanged(block, "row", stride) for stride in far]
     shift = far[0].bit_length() - 1
-    places = [row >> shift] + [(row ^ stride) >> shift for stride in far]
+    places = [scalar((row ^ stride) >> shift) for stride in (0, *far)]
     months = lax.axis_size("tm")
     month = lax.axis_index("tm")
 
     wide = jax.ShapeDtypeStruct((rhs, count), jnp.float32)
     params = pltpu.CompilerParams(vmem_limit_bytes=8 << 20)
-    product, own_low = pl.pallas_call(
+    product = pl.pallas_call(
         first_kernel,
-        in_specs=[SMEM] + [VMEM] * 4,
-        out_specs=[VMEM] * 2,
-        out_shape=[wide, low_type],
+        in_specs=[SMEM] * 2 + [VMEM] * 4,
+        out_specs=VMEM,
+        out_shape=wide,
         compiler_params=params,
         cost_estimate=pl.CostEstimate(flops=2 * rhs * count * width, bytes_accessed=2 * count * width, transcendentals=0),
         name="first",
-    )(jnp.stack(places[:2]), block, blocks[0], own_low, normal[0])
-    before = lax.ppermute(own_low, "tm", [(i, i + 1) for i in range(months - 1)])
-    after = lax.ppermute(own_low, "tm", [(i + 1, i) for i in range(months - 1)])
+    )(*places[:2], block, blocks[0], normal[0], jnp.concatenate(places))
+    pairs = [[(i, i + 1) for i in range(first, months - 1, 2)] for first in (0, 1)]
+    before, after = (lax.ppermute(dirs, "tm", [way for i, j in pair for way in ((i, j), (j, i))]) for pair in pairs)
     late = blocks[1:]
+    has_before = (month ^ 1) < months
+    has_after = (month > 0) & ((month & 1 == 0) | (month < months - 1))
     image, grams = pl.pallas_call(
         functools.partial(image_kernel, len(late)),
-        in_specs=[SMEM] * 2 + [VMEM] * (len(late) + 7),
+        in_specs=[SMEM] * len(late) + [VMEM] * len(late) + [SMEM] * 2 + [VMEM] * 7,
         out_specs=[VMEM] * 2,
         out_shape=[wide, jax.ShapeDtypeStruct((rhs, 6 * rhs), jnp.float32)],
         compiler_params=params,
         name="image",
     )(
-        jnp.stack(places[2:]), jnp.stack([month > 0, month < months - 1]).astype(jnp.int32),
-        *late, normal[0], product, dirs, resid, before, after, weights[None],
+        *places[2:], *late, scalar(has_before), scalar(has_after),
+        normal[0], product, dirs, resid, before, after, weights[None],
     )
     steps = [(axis, strides) for axis in ("row", "tm") for strides in rounds(lax.axis_size(axis))]
     parts = [grams]

time: 43 us -> 35.6 us (0.83)
  waiting for transfers between devices: 11.3 us -> 6.85 us
  starting transfers between devices: 19.8 us -> 18.1 us
  Pallas kernels: 9.84 us -> 8.21 us
  local copies, waits for them, and re-layouts: 0.85 us -> 1.46 us
    ppermute x11, waiting for transfers between devices: 9.81 us -> 6.83 us  [exchanged(): lax.ppermute(value, axis, [(i, i ^ stride) for i in range(lax.axis_size(a...]
    ppermute x11, starting transfers between devices: 13.9 us -> 12 us  [exchanged(): lax.ppermute(value, axis, [(i, i ^ stride) for i in range(lax.axis_size(a...]
    ppermute x2, waiting for transfers between devices: 1.49 us -> 0.02 us  [local(): lax.ppermute(dirs, 'tm', [way for i, j in pair for way in ((i, j), (j, i))])]
    pallas_call x3 -> x2, Pallas kernels: 3.36 us -> 2.27 us  [the longest x1 2.26 us: local(): pl.pallas_call(first_kernel, in_specs=[SMEM] * 2 + [VMEM] * 4, out_specs=...]
    unnamed x12, local copies, waits for them, and re-layouts: 0.85 us -> 1.46 us
    pallas_call x1, Pallas kernels: 3.21 us -> 2.68 us  [local(): pl.pallas_call(functools.partial(image_kernel, len(late)), in_specs=[SMEM...]
  transfers between devices with their start and end apart: 13 -> 13, of which waited for: 9 -> 9; matrix products, arithmetic and copies ran while one was open for 1% -> 0% of each run, Pallas kernels for 7% -> 6%
where the time goes in v2:
time: 35.6 us; the launch traced here: 35.4 us
  starting transfers between devices  18.1 us (51%)
  Pallas kernels  8.21 us (23%)
  waiting for transfers between devices  6.85 us (19%)
  local copies, waits for them, and re-layouts  1.46 us (4%)
  between operations  0.69 us (2%)
    ppermute x11, starting transfers between devices, exchanged(): lax.ppermute(value, axis, [(i, i ^ stride) for i in range(lax.axis_size(a...  12 us
    ppermute x11, waiting for transfers between devices, exchanged(): lax.ppermute(value, axis, [(i, i ^ stride) for i in range(lax.axis_size(a...  6.83 us
    ppermute x2, starting transfers between devices, local(): lax.ppermute(dirs, 'tm', [way for i, j in pair for way in ((i, j), (j, i))])  6.13 us
    pallas_call x1, Pallas kernels, local(): pl.pallas_call(update_kernel, in_specs=[VMEM] * (len(parts) + 4), out_spe...  3.26 us
    pallas_call x1, Pallas kernels, local(): pl.pallas_call(functools.partial(image_kernel, len(late)), in_specs=[SMEM...  2.68 us
    pallas_call x1, Pallas kernels, local(): pl.pallas_call(first_kernel, in_specs=[SMEM] * 2 + [VMEM] * 4, out_specs=...  2.26 us
    unnamed x12, local copies, waits for them, and re-layouts  1.46 us
  transfers between devices with their start and end apart: 13, of which 9 were waited for; matrix products, arithmetic and copies ran while one was open for 0% of the time, Pallas kernels for 6%

profile of v2, /device:TPU:0, one launch (start us, length us, event | category | flops | bytes accessed | tf_op | source)
XLA Modules:
  0.0 35.4 jit_solution(15347963566381984804)
XLA Ops:
  0.6 0.5 %collective-permute-start = (f32[16,1024]{1,0:T(8,128)}, f32[16,1024]{1,0:T(8,128)S(1)}, u32[]{:S(2)}, u32[]{:S(2)}) collective-permute-start(f32[16,1024]{1,0:T(8,128)} %bitcast.19), channel_id=1, source_target_pairs={{0,1},{1,0},{2,3},{3,2},{4,5},{5,4},{6,7},{7,6},{8,9},{9,8},{10,11... | collective-permute-start | bytes 196616 | tf_op jit(solution)/shard_map/ppermute | solution.py:112
  1.1 0.7 %collective-permute-start.5 = (f32[16,1024]{1,0:T(8,128)}, f32[16,1024]{1,0:T(8,128)S(1)}, u32[]{:S(2)}, u32[]{:S(2)}) collective-permute-start(f32[16,1024]{1,0:T(8,128)} %bitcast.20), channel_id=1, source_target_pairs={{8,16},{16,8},{9,17},{17,9},{10,18},{18,10},{11,19},{19,11},{12,20... | collective-permute-start | bytes 196616 | tf_op jit(solution)/shard_map/ppermute | solution.py:168
  1.8 5.5 %collective-permute-start.4 = (f32[16,1024]{1,0:T(8,128)}, f32[16,1024]{1,0:T(8,128)S(1)}, u32[]{:S(2)}, u32[]{:S(2)}) collective-permute-start(f32[16,1024]{1,0:T(8,128)} %bitcast.21), channel_id=1, source_target_pairs={{0,8},{8,0},{16,24},{24,16},{1,9},{9,1},{17,25},{25,17},{2,10},{10... | collective-permute-start | bytes 196616 | tf_op jit(solution)/shard_map/ppermute | solution.py:168
  7.3 0.0 copy-start
  7.3 0.0 collective-permute-done.refs_4_
  7.3 0.0 copy-start.1
  7.3 1.0 %copy-done.1 = f32[1,16,1024]{2,1,0:T(8,128)S(1)} copy-done((f32[1,16,1024]{2,1,0:T(8,128)S(1)}, f32[1,16,1024]{2,1,0:T(8,128)}, u32[]{:S(2)}) %copy-start.1) | copy-done | bytes 65560
  8.3 0.0 copy-start.2
  8.3 0.0 copy-start.3
  8.3 0.0 copy-start.5
  8.3 1.6 %collective-permute-start.3 = (bf16[16,2048]{1,0:T(8,128)(2,1)S(1)}, bf16[16,2048]{1,0:T(8,128)(2,1)S(1)}, u32[]{:S(2)}, u32[]{:S(2)}) collective-permute-start(bf16[16,2048]{1,0:T(8,128)(2,1)S(1)} %place.1.block_ref), channel_id=1, source_target_pairs={{0,2},{1,3},{2,0},{3,1},{4,6},{5,7},{6,4},{7,5},{8,10},{9,11},{10,... | collective-permute-start | bytes 196616 | tf_op jit(solution)/shard_map/ppermute | solution.py:112
  9.9 1.5 %collective-permute-start.2 = (bf16[16,2048]{1,0:T(8,128)(2,1)S(1)}, bf16[16,2048]{1,0:T(8,128)(2,1)S(1)}, u32[]{:S(2)}, u32[]{:S(2)}) collective-permute-start(bf16[16,2048]{1,0:T(8,128)(2,1)S(1)} %place.1.block_ref), channel_id=1, source_target_pairs={{0,6},{1,7},{2,4},{3,5},{4,2},{5,3},{6,0},{7,1},{8,14},{9,15},{10,... | collective-permute-start | bytes 196616 | tf_op jit(solution)/shard_map/ppermute | solution.py:112
  11.4 0.5 %collective-permute-start.1 = (bf16[16,2048]{1,0:T(8,128)(2,1)S(1)}, bf16[16,2048]{1,0:T(8,128)(2,1)S(1)}, u32[]{:S(2)}, u32[]{:S(2)}) collective-permute-start(bf16[16,2048]{1,0:T(8,128)(2,1)S(1)} %place.1.block_ref), channel_id=1, source_target_pairs={{0,4},{1,5},{2,6},{3,7},{4,0},{5,1},{6,2},{7,3},{8,12},{9,13},{10,... | collective-permute-start | bytes 196616 | tf_op jit(solution)/shard_map/ppermute | solution.py:112
  11.9 0.1 pad_add_fusion._
  11.9 0.0 copy-start.4
  11.9 0.7 %collective-permute-done.3.next_ref = bf16[16,2048]{1,0:T(8,128)(2,1)S(1)} collective-permute-done((bf16[16,2048]{1,0:T(8,128)(2,1)S(1)}, bf16[16,2048]{1,0:T(8,128)(2,1)S(1)}, u32[]{:S(2)}, u32[]{:S(2)}) %collective-permute-start.3) | collective-permute-done | bytes 65568 | tf_op jit(solution)/shard_map/ppermute | solution.py:112
  12.6 0.5 %copy-done = bf16[1,1024,8192]{2,1,0:T(8,128)(2,1)S(1)} copy-done((bf16[1,1024,8192]{2,1,0:T(8,128)(2,1)S(1)}, bf16[1,1024,8192]{2,1,0:T(8,128)(2,1)}, u32[]{:S(2)}) %copy-start) | copy-done | bytes 16777240
  13.1 2.3 %first.1.refs_7_ = f32[16,1024]{1,0:T(8,128)S(1)} custom-call(s32[1]{0:T(128)} %bitcast.8.place_ref, s32[1]{0:T(128)} %bitcast.9.next_place_ref, bf16[16,2048]{1,0:T(8,128)(2,1)S(1)} %place.1.block_ref, bf16[16,2048]{1,0:T(8,128)(2,1)S(1)} %collective-permute-done.3.next_ref, bf16[1024,8192]{1,0:T(8,128)(2,1)S(1)} %bitcast.17, s32[4]{0:T(128)S(1)} %pad_add_fusion._), custom_call_target="tpu_custom_call" | custom-call | flops 67108864 | bytes 4194304 | tf_op jit(solution)/shard_map/first/pallas_call | solution.py:158
  15.4 0.0 collective-permute-done.5.refs_11_
  15.4 0.0 collective-permute-done.4.refs_10_
  15.4 0.0 collective-permute-done.2.refs_3_
  15.4 0.6 %collective-permute-done.1.refs_2_ = bf16[16,2048]{1,0:T(8,128)(2,1)S(1)} collective-permute-done((bf16[16,2048]{1,0:T(8,128)(2,1)S(1)}, bf16[16,2048]{1,0:T(8,128)(2,1)S(1)}, u32[]{:S(2)}, u32[]{:S(2)}) %collective-permute-start.1) | collective-permute-done | bytes 65568 | tf_op jit(solution)/shard_map/ppermute | solution.py:112
  16.0 0.0 copy-done.2
  16.0 0.0 copy-done.3
  16.0 0.0 copy-done.5
  16.0 2.7 %image.1 = (f32[16,1024]{1,0:T(8,128)S(1)}, f32[16,96]{1,0:T(8,128)S(1)}) custom-call(s32[1]{0:T(128)} %bitcast.refs_0_, s32[1]{0:T(128)} %bitcast.1.refs_1_, bf16[16,2048]{1,0:T(8,128)(2,1)S(1)} %collective-permute-done.1.refs_2_, bf16[16,2048]{1,0:T(8,128)(2,1)S(1)} %collective-permute-done.2.refs_3_, s32[1]{0:T(128)} %bitcast.6.refs_4_, ...), custom_call_target="tpu_custom_call" | custom-call | tf_op jit(solution)/shard_map/image/pallas_call | solution.py:172
  18.7 0.0 collective-permute-start.6
  18.7 1.2 %collective-permute-done.6 = f32[16,96]{1,0:T(8,128)S(1)} collective-permute-done((f32[16,96]{1,0:T(8,128)S(1)}, f32[16,96]{1,0:T(8,128)S(1)}, u32[]{:S(2)}, u32[]{:S(2)}) %collective-permute-start.6) | collective-permute-done | bytes 6176 | tf_op jit(solution)/shard_map/ppermute | solution.py:112
  19.9 1.9 %collective-permute-start.9 = (f32[16,96]{1,0:T(8,128)S(1)}, f32[16,96]{1,0:T(8,128)S(1)}, u32[]{:S(2)}, u32[]{:S(2)}) collective-permute-start(f32[16,96]{1,0:T(8,128)S(1)} %add.12), channel_id=1, source_target_pairs={{0,6},{1,7},{2,4},{3,5},{4,2},{5,3},{6,0},{7,1},{8,14},{9,15},{10,... | collective-permute-start | bytes 18440 | tf_op jit(solution)/shard_map/ppermute | solution.py:112
  21.7 0.7 %collective-permute-start.8 = (f32[16,96]{1,0:T(8,128)S(1)}, f32[16,96]{1,0:T(8,128)S(1)}, u32[]{:S(2)}, u32[]{:S(2)}) collective-permute-start(f32[16,96]{1,0:T(8,128)S(1)} %add.12), channel_id=1, source_target_pairs={{0,4},{1,5},{2,6},{3,7},{4,0},{5,1},{6,2},{7,3},{8,12},{9,13},{10,... | collective-permute-start | bytes 18440 | tf_op jit(solution)/shard_map/ppermute | solution.py:112
  22.5 0.9 %collective-permute-start.7 = (f32[16,96]{1,0:T(8,128)S(1)}, f32[16,96]{1,0:T(8,128)S(1)}, u32[]{:S(2)}, u32[]{:S(2)}) collective-permute-start(f32[16,96]{1,0:T(8,128)S(1)} %add.12), channel_id=1, source_target_pairs={{0,2},{1,3},{2,0},{3,1},{4,6},{5,7},{6,4},{7,5},{8,10},{9,11},{10,... | collective-permute-start | bytes 18440 | tf_op jit(solution)/shard_map/ppermute | solution.py:112
  23.3 1.1 %collective-permute-done.9 = f32[16,96]{1,0:T(8,128)S(1)} collective-permute-done((f32[16,96]{1,0:T(8,128)S(1)}, f32[16,96]{1,0:T(8,128)S(1)}, u32[]{:S(2)}, u32[]{:S(2)}) %collective-permute-start.9) | collective-permute-done | bytes 6176 | tf_op jit(solution)/shard_map/ppermute | solution.py:112
  24.4 1.0 %collective-permute-done.8 = f32[16,96]{1,0:T(8,128)S(1)} collective-permute-done((f32[16,96]{1,0:T(8,128)S(1)}, f32[16,96]{1,0:T(8,128)S(1)}, u32[]{:S(2)}, u32[]{:S(2)}) %collective-permute-start.8) | collective-permute-done | bytes 6176 | tf_op jit(solution)/shard_map/ppermute | solution.py:112
  25.4 0.7 %collective-permute-done.7 = f32[16,96]{1,0:T(8,128)S(1)} collective-permute-done((f32[16,96]{1,0:T(8,128)S(1)}, f32[16,96]{1,0:T(8,128)S(1)}, u32[]{:S(2)}, u32[]{:S(2)}) %collective-permute-start.7) | collective-permute-done | bytes 6176 | tf_op jit(solution)/shard_map/ppermute | solution.py:112
  26.1 1.3 %collective-permute-start.12 = (f32[16,96]{1,0:T(8,128)S(1)}, f32[16,96]{1,0:T(8,128)S(1)}, u32[]{:S(2)}, u32[]{:S(2)}) collective-permute-start(f32[16,96]{1,0:T(8,128)S(1)} %add_add_fusion.refs_0_), channel_id=1, source_target_pairs={{0,24},{8,16},{16,8},{24,0},{1,25},{9,17},{17,9},{25,1},{2,26},{10... | collective-permute-start | bytes 18440 | tf_op jit(solution)/shard_map/ppermute | solution.py:112
  27.5 0.6 %collective-permute-start.11 = (f32[16,96]{1,0:T(8,128)S(1)}, f32[16,96]{1,0:T(8,128)S(1)}, u32[]{:S(2)}, u32[]{:S(2)}) collective-permute-start(f32[16,96]{1,0:T(8,128)S(1)} %add_add_fusion.refs_0_), channel_id=1, source_target_pairs={{0,16},{8,24},{16,0},{24,8},{1,17},{9,25},{17,1},{25,9},{2,18},{10... | collective-permute-start | bytes 18440 | tf_op jit(solution)/shard_map/ppermute | solution.py:112
  28.0 2.5 %collective-permute-start.10 = (f32[16,96]{1,0:T(8,128)S(1)}, f32[16,96]{1,0:T(8,128)S(1)}, u32[]{:S(2)}, u32[]{:S(2)}) collective-permute-start(f32[16,96]{1,0:T(8,128)S(1)} %add_add_fusion.refs_0_), channel_id=1, source_target_pairs={{0,8},{8,0},{16,24},{24,16},{1,9},{9,1},{17,25},{25,17},{2,10},{10... | collective-permute-start | bytes 18440 | tf_op jit(solution)/shard_map/ppermute | solution.py:112
  30.5 1.1 %collective-permute-done.12.refs_3_ = f32[16,96]{1,0:T(8,128)S(1)} collective-permute-done((f32[16,96]{1,0:T(8,128)S(1)}, f32[16,96]{1,0:T(8,128)S(1)}, u32[]{:S(2)}, u32[]{:S(2)}) %collective-permute-start.12) | collective-permute-done | bytes 6176 | tf_op jit(solution)/shard_map/ppermute | solution.py:112
  31.6 0.4 %collective-permute-done.11.refs_2_ = f32[16,96]{1,0:T(8,128)S(1)} collective-permute-done((f32[16,96]{1,0:T(8,128)S(1)}, f32[16,96]{1,0:T(8,128)S(1)}, u32[]{:S(2)}, u32[]{:S(2)}) %collective-permute-start.11) | collective-permute-done | bytes 6176 | tf_op jit(solution)/shard_map/ppermute | solution.py:112
  32.0 0.1 collective-permute-done.10.refs_1_
  32.1 0.0 copy-done.4
  32.1 3.3 %update.1 = (f32[16,1024]{1,0:T(8,128)}, f32[16,1024]{1,0:T(8,128)}, f32[16,1024]{1,0:T(8,128)}) custom-call(f32[16,96]{1,0:T(8,128)S(1)} %add_add_fusion.refs_0_, f32[16,96]{1,0:T(8,128)S(1)} %collective-permute-done.10.refs_1_, f32[16,96]{1,0:T(8,128)S(1)} %collective-permute-done.11.refs_2_, f32[16,96]{1,0:T(8,128)S(1)} %collective-permute-done.12.refs_3_, ...), custom_call_target="tpu_custom_call" | custom-call | tf_op jit(solution)/shard_map/update/pallas_call | solution.py:188
  (3 shorter events, 0.0 us)
Async XLA Ops:
  0.6 6.7 %collective-permute-start = (f32[16,1024]{1,0:T(8,128)}, f32[16,1024]{1,0:T(8,128)S(1)}, u32[]{:S(2)}, u32[]{:S(2)}) collective-permute-start(f32[16,1024]{1,0:T(8,128)} %bitcast.19), channel_id=1, source_target_pairs={{0,1},{1,0},{2,3},{3,2},{4,5},{5,4},{6,7},{7,6},{8,9},{9,8},{10,11... | collective-permute-start | bytes 196616 | tf_op jit(solution)/shard_map/ppermute | solution.py:112
  1.1 14.2 %collective-permute-start.5 = (f32[16,1024]{1,0:T(8,128)}, f32[16,1024]{1,0:T(8,128)S(1)}, u32[]{:S(2)}, u32[]{:S(2)}) collective-permute-start(f32[16,1024]{1,0:T(8,128)} %bitcast.20), channel_id=1, source_target_pairs={{8,16},{16,8},{9,17},{17,9},{10,18},{18,10},{11,19},{19,11},{12,20... | collective-permute-start | bytes 196616 | tf_op jit(solution)/shard_map/ppermute | solution.py:168
  1.8 13.6 %collective-permute-start.4 = (f32[16,1024]{1,0:T(8,128)}, f32[16,1024]{1,0:T(8,128)S(1)}, u32[]{:S(2)}, u32[]{:S(2)}) collective-permute-start(f32[16,1024]{1,0:T(8,128)} %bitcast.21), channel_id=1, source_target_pairs={{0,8},{8,0},{16,24},{24,16},{1,9},{9,1},{17,25},{25,17},{2,10},{10... | collective-permute-start | bytes 196616 | tf_op jit(solution)/shard_map/ppermute | solution.py:168
  7.3 5.8 %copy-start = (bf16[1,1024,8192]{2,1,0:T(8,128)(2,1)S(1)}, bf16[1,1024,8192]{2,1,0:T(8,128)(2,1)}, u32[]{:S(2)}) copy-start(bf16[1,1024,8192]{2,1,0:T(8,128)(2,1)} %param.8) | copy-start | bytes 50331652
  7.3 1.0 %copy-start.1 = (f32[1,16,1024]{2,1,0:T(8,128)S(1)}, f32[1,16,1024]{2,1,0:T(8,128)}, u32[]{:S(2)}) copy-start(f32[1,16,1024]{2,1,0:T(8,128)} %param.7) | copy-start | bytes 196612
  8.3 7.7 %copy-start.2 = (f32[1,16,1024]{2,1,0:T(8,128)S(1)}, f32[1,16,1024]{2,1,0:T(8,128)}, u32[]{:S(2)}) copy-start(f32[1,16,1024]{2,1,0:T(8,128)} %param.7) | copy-start | bytes 196612
  8.3 7.7 %copy-start.3 = (f32[1,16,1024]{2,1,0:T(8,128)S(1)}, f32[1,16,1024]{2,1,0:T(8,128)}, u32[]{:S(2)}) copy-start(f32[1,16,1024]{2,1,0:T(8,128)} %param.6) | copy-start | bytes 196612
  8.3 7.7 %copy-start.5 = (f32[1024]{0:T(1024)S(1)}, f32[1024]{0:T(1024)}, u32[]{:S(2)}) copy-start(f32[1024]{0:T(1024)} %param.9) | copy-start | bytes 12292
  8.3 4.3 %collective-permute-start.3 = (bf16[16,2048]{1,0:T(8,128)(2,1)S(1)}, bf16[16,2048]{1,0:T(8,128)(2,1)S(1)}, u32[]{:S(2)}, u32[]{:S(2)}) collective-permute-start(bf16[16,2048]{1,0:T(8,128)(2,1)S(1)} %place.1.block_ref), channel_id=1, source_target_pairs={{0,2},{1,3},{2,0},{3,1},{4,6},{5,7},{6,4},{7,5},{8,10},{9,11},{10,... | collective-permute-start | bytes 196616 | tf_op jit(solution)/shard_map/ppermute | solution.py:112
  9.9 5.5 %collective-permute-start.2 = (bf16[16,2048]{1,0:T(8,128)(2,1)S(1)}, bf16[16,2048]{1,0:T(8,128)(2,1)S(1)}, u32[]{:S(2)}, u32[]{:S(2)}) collective-permute-start(bf16[16,2048]{1,0:T(8,128)(2,1)S(1)} %place.1.block_ref), channel_id=1, source_target_pairs={{0,6},{1,7},{2,4},{3,5},{4,2},{5,3},{6,0},{7,1},{8,14},{9,15},{10,... | collective-permute-start | bytes 196616 | tf_op jit(solution)/shard_map/ppermute | solution.py:112
  11.4 4.6 %collective-permute-start.1 = (bf16[16,2048]{1,0:T(8,128)(2,1)S(1)}, bf16[16,2048]{1,0:T(8,128)(2,1)S(1)}, u32[]{:S(2)}, u32[]{:S(2)}) collective-permute-start(bf16[16,2048]{1,0:T(8,128)(2,1)S(1)} %place.1.block_ref), channel_id=1, source_target_pairs={{0,4},{1,5},{2,6},{3,7},{4,0},{5,1},{6,2},{7,3},{8,12},{9,13},{10,... | collective-permute-start | bytes 196616 | tf_op jit(solution)/shard_map/ppermute | solution.py:112
  11.9 20.2 %copy-start.4 = (f32[1,16,1024]{2,1,0:T(8,128)S(1)}, f32[1,16,1024]{2,1,0:T(8,128)}, u32[]{:S(2)}) copy-start(f32[1,16,1024]{2,1,0:T(8,128)} %param.5) | copy-start | bytes 196612
  18.7 1.2 %collective-permute-start.6 = (f32[16,96]{1,0:T(8,128)S(1)}, f32[16,96]{1,0:T(8,128)S(1)}, u32[]{:S(2)}, u32[]{:S(2)}) collective-permute-start(f32[16,96]{1,0:T(8,128)S(1)} %get-tuple-element.8), channel_id=1, source_target_pairs={{0,1},{1,0},{2,3},{3,2},{4,5},{5,4},{6,7},{7,6},{8,9},{9,8},{10,11... | collective-permute-start | bytes 18440 | tf_op jit(solution)/shard_map/ppermute | solution.py:112
  19.9 4.6 %collective-permute-start.9 = (f32[16,96]{1,0:T(8,128)S(1)}, f32[16,96]{1,0:T(8,128)S(1)}, u32[]{:S(2)}, u32[]{:S(2)}) collective-permute-start(f32[16,96]{1,0:T(8,128)S(1)} %add.12), channel_id=1, source_target_pairs={{0,6},{1,7},{2,4},{3,5},{4,2},{5,3},{6,0},{7,1},{8,14},{9,15},{10,... | collective-permute-start | bytes 18440 | tf_op jit(solution)/shard_map/ppermute | solution.py:112
  21.7 3.7 %collective-permute-start.8 = (f32[16,96]{1,0:T(8,128)S(1)}, f32[16,96]{1,0:T(8,128)S(1)}, u32[]{:S(2)}, u32[]{:S(2)}) collective-permute-start(f32[16,96]{1,0:T(8,128)S(1)} %add.12), channel_id=1, source_target_pairs={{0,4},{1,5},{2,6},{3,7},{4,0},{5,1},{6,2},{7,3},{8,12},{9,13},{10,... | collective-permute-start | bytes 18440 | tf_op jit(solution)/shard_map/ppermute | solution.py:112
  22.5 3.7 %collective-permute-start.7 = (f32[16,96]{1,0:T(8,128)S(1)}, f32[16,96]{1,0:T(8,128)S(1)}, u32[]{:S(2)}, u32[]{:S(2)}) collective-permute-start(f32[16,96]{1,0:T(8,128)S(1)} %add.12), channel_id=1, source_target_pairs={{0,2},{1,3},{2,0},{3,1},{4,6},{5,7},{6,4},{7,5},{8,10},{9,11},{10,... | collective-permute-start | bytes 18440 | tf_op jit(solution)/shard_map/ppermute | solution.py:112
  26.1 5.4 %collective-permute-start.12 = (f32[16,96]{1,0:T(8,128)S(1)}, f32[16,96]{1,0:T(8,128)S(1)}, u32[]{:S(2)}, u32[]{:S(2)}) collective-permute-start(f32[16,96]{1,0:T(8,128)S(1)} %add_add_fusion.refs_0_), channel_id=1, source_target_pairs={{0,24},{8,16},{16,8},{24,0},{1,25},{9,17},{17,9},{25,1},{2,26},{10... | collective-permute-start | bytes 18440 | tf_op jit(solution)/shard_map/ppermute | solution.py:112
  27.5 4.5 %collective-permute-start.11 = (f32[16,96]{1,0:T(8,128)S(1)}, f32[16,96]{1,0:T(8,128)S(1)}, u32[]{:S(2)}, u32[]{:S(2)}) collective-permute-start(f32[16,96]{1,0:T(8,128)S(1)} %add_add_fusion.refs_0_), channel_id=1, source_target_pairs={{0,16},{8,24},{16,0},{24,8},{1,17},{9,25},{17,1},{25,9},{2,18},{10... | collective-permute-start | bytes 18440 | tf_op jit(solution)/shard_map/ppermute | solution.py:112
  28.0 4.1 %collective-permute-start.10 = (f32[16,96]{1,0:T(8,128)S(1)}, f32[16,96]{1,0:T(8,128)S(1)}, u32[]{:S(2)}, u32[]{:S(2)}) collective-permute-start(f32[16,96]{1,0:T(8,128)S(1)} %add_add_fusion.refs_0_), channel_id=1, source_target_pairs={{0,8},{8,0},{16,24},{24,16},{1,9},{9,1},{17,25},{25,17},{2,10},{10... | collective-permute-start | bytes 18440 | tf_op jit(solution)/shard_map/ppermute | solution.py:112

commit v3 on v2

--- a/solution.py
+++ b/solution.py
@@ -13,6 +13,8 @@
 VMEM = pl.BlockSpec(memory_space=pltpu.VMEM)
 HBM = pl.BlockSpec(memory_space=pltpu.HBM)
 TILE = 256
+SCALE_ROWS = 8
+SMALLEST = 2.0**-126
 
 
 def dot_nt(left, right):
@@ -21,6 +23,10 @@
 
 def dot_nn(left, right):
     return jnp.dot(left, right, precision=HIGH, preferred_element_type=jnp.float32)
+
+
+def mark_kernel(_, out_ref):
+    out_ref[...] = jnp.zeros(out_ref.shape, out_ref.dtype)
 
 
 def rounded(ref):
@@ -67,45 +73,84 @@
     image_ref[...] = sum_ref[...] + weights_ref[...] * coupled
     product_of(places, blocks, slab_ref, image_ref, image_ref)
     image = image_ref[...]
-    left = jnp.concatenate([resid, dirs, image], axis=0)
-    right = jnp.concatenate([resid, image], axis=0)
-    grams = dot_nt(left, right)
     rhs = resid.shape[0]
-    grams_ref[...] = jnp.concatenate([grams[:rhs], grams[rhs : 2 * rhs], grams[2 * rhs :]], axis=1)
+    straight = dot_nt(jnp.concatenate([resid, dirs], axis=0), jnp.concatenate([resid, image], axis=0))
+    scale = jnp.maximum(jnp.max(jnp.abs(image), keepdims=True), SMALLEST)
+    scaled = image * (1.0 / scale)
+    across = dot_nt(scaled, jnp.concatenate([resid, scaled], axis=0))
+    grams_ref[:rhs, :] = jnp.concatenate([straight[:rhs], straight[rhs:], across], axis=1)
+    grams_ref[rhs:, :] = jnp.broadcast_to(scale, (SCALE_ROWS, 6 * rhs))
+
+
+def total(refs):
+    rhs = refs[0].shape[0] - SCALE_ROWS
+    scales = [ref[rhs : rhs + 1, :] for ref in refs]
+    scale = functools.reduce(jnp.maximum, scales)
+    block = lax.broadcasted_iota(jnp.int32, scale.shape, 1) // rhs
+    out = 0.0
+    for ref, own in zip(refs, scales, strict=True):
+        ratio = own / scale
+        factor = jnp.where(block == 5, ratio * ratio, jnp.where(block == 4, ratio, 1.0))
+        out = out + ref[:rhs, :] * factor
+    return out, scale
+
+
+def total_kernel(*refs):
+    *parts, out_ref = refs
+    grams, scale = total(parts)
+    out_ref[: grams.shape[0], :] = grams
+    out_ref[grams.shape[0] :, :] = jnp.broadcast_to(scale, (SCALE_ROWS, grams.shape[1]))
+
+
+def reciprocal(value):
+    guess = pl.reciprocal(value, approx=True)
+    for _ in range(2):
+        guess = guess * (2.0 - value * guess)
+    return guess
 
 
 def right_divide(*systems):
     size = systems[0][0].shape[0]
     works = [jnp.concatenate(system, axis=0) for system in systems]
     lane = lax.broadcasted_iota(jnp.int32, works[0].shape, 1)
-    for k in range(size):
+    for k in range(0, size, 2):
+        here, after = lane == k, lane == k + 1
         for i, work in enumerate(works):
-            row = work[k : k + 1, :]
-            column = work[:, k : k + 1]
-            inverse = 1.0 / work[k : k + 1, k : k + 1]
-            scaled = jnp.where(lane[:1] == k, -inverse, row * inverse)
-            works[i] = jnp.where(lane == k, 0.0, work) - column * scaled
+            first = jnp.broadcast_to(work[:, k : k + 1], work.shape)
+            second = jnp.broadcast_to(work[:, k + 1 : k + 2], work.shape)
+            over = first[k : k + 1]
+            under = first[k + 1 : k + 2]
+            beside = second[k : k + 1]
+            inverse = reciprocal(over)
+            ratio = under * inverse
+            inverse_next = reciprocal(second[k + 1 : k + 2] - ratio * beside)
+            top = jnp.where(here[:1], -1.0, jnp.where(after[:1], 0.0, work[k : k + 1]))
+            low = jnp.where(here[:1], 0.0, jnp.where(after[:1], -1.0, work[k + 1 : k + 2]))
+            low = (low - ratio * top) * inverse_next
+            top = (top - beside * low) * inverse
+            works[i] = jnp.where(here | after, 0.0, work) - first * top - second * low
     return [work[size:] for work in works]
 
 
 def update_kernel(*refs):
     *gram_refs, solution_ref, resid_ref, dirs_ref, image_ref, next_solution_ref, next_resid_ref, next_dirs_ref = refs
-    grams = sum((ref[...] for ref in gram_refs[1:]), gram_refs[0][...])
+    grams, scale = total(gram_refs)
     rhs = grams.shape[0]
-    rr, rq, _, dq, qr, qq = (grams[:, i * rhs : (i + 1) * rhs] for i in range(6))
+    rr, _, _, dq, qr, qq = (grams[:, i * rhs : (i + 1) * rhs] for i in range(6))
     old = 0.5 * (rr + rr.T)
     curvature = 0.5 * (dq + dq.T)
     rows = lax.broadcasted_iota(jnp.int32, (rhs, rhs), 0)
     cols = lax.broadcasted_iota(jnp.int32, (rhs, rhs), 1)
     unit = jnp.where(rows == cols, 1.0, 0.0).astype(jnp.float32)
     alpha_t, old_inverse = right_divide((curvature, old), (old, unit))
-    new = rr - dot_nn(alpha_t, qr) + dot_nt(dot_nn(alpha_t, qq) - rq, alpha_t)
-    beta_t = dot_nn(new, old_inverse)
+    scaled_t = alpha_t * scale[:, :rhs]
     dirs = dirs_ref[...]
+    apart = dot_nn(old_inverse, dirs)
+    new = rr - dot_nn(scaled_t, qr) + dot_nt(dot_nn(scaled_t, qq) - qr.T, scaled_t)
     next_resid = resid_ref[...] - dot_nn(alpha_t, image_ref[...])
     next_resid_ref[...] = next_resid
     next_solution_ref[...] = solution_ref[...] + dot_nn(alpha_t, dirs)
-    next_dirs_ref[...] = next_resid + dot_nn(beta_t, dirs)
+    next_dirs_ref[...] = next_resid + dot_nn(new, apart)
 
 
 def exchanged(value, axis, stride):
@@ -129,7 +174,7 @@
     slots = [scalar(((index ^ stride) >> shift) & (count - 1)) for stride in (0, *strides)]
     return pl.pallas_call(
         functools.partial(place_kernel, count),
-        in_specs=[SMEM] * count + [HBM] + [VMEM] * count,
+        in_specs=[SMEM] * count + [VMEM] * (count + 1),
         out_specs=VMEM,
         out_shape=jax.ShapeDtypeStruct((block.shape[0], count * block.shape[1]), jnp.bfloat16),
         compiler_params=pltpu.CompilerParams(vmem_limit_bytes=2 << 20),
@@ -141,11 +186,19 @@
     rhs, count = direction.shape[1:]
     dirs, resid = direction[0], residual[0]
     slab = pltpu.with_memory_space_constraint(normal[0], pltpu.HBM)
+    mark = pl.pallas_call(
+        mark_kernel,
+        in_specs=[HBM],
+        out_specs=VMEM,
+        out_shape=jax.ShapeDtypeStruct((8, 128), jnp.float32),
+        compiler_params=pltpu.CompilerParams(vmem_limit_bytes=2 << 20),
+        name="mark",
+    )(slab)
     row = lax.axis_index("row")
     *near, far = rounds(lax.axis_size("row"))
     block = dirs
     for strides in near:
-        block = gathered(block, row, strides, slab)
+        block = gathered(block, row, strides, mark)
     width = block.shape[1]
     blocks = [exchanged(block, "row", stride) for stride in far]
     shift = far[0].bit_length() - 1
@@ -154,6 +207,7 @@
     month = lax.axis_index("tm")
 
     wide = jax.ShapeDtypeStruct((rhs, count), jnp.float32)
+    gram_type = jax.ShapeDtypeStruct((rhs + SCALE_ROWS, 6 * rhs), jnp.float32)
     params = pltpu.CompilerParams(vmem_limit_bytes=8 << 20)
     product = pl.pallas_call(
         first_kernel,
@@ -173,7 +227,7 @@
         functools.partial(image_kernel, len(late)),
         in_specs=[SMEM] * len(late) + [VMEM] * len(late) + [SMEM] * 2 + [VMEM] * 7,
         out_specs=[VMEM] * 2,
-        out_shape=[wide, jax.ShapeDtypeStruct((rhs, 6 * rhs), jnp.float32)],
+        out_shape=[wide, gram_type],
         compiler_params=params,
         name="image",
     )(
@@ -183,8 +237,16 @@
     steps = [(axis, strides) for axis in ("row", "tm") for strides in rounds(lax.axis_size(axis))]
     parts = [grams]
     for axis, strides in steps:
-        total = functools.reduce(jnp.add, parts)
-        parts = [total] + [exchanged(total, axis, stride) for stride in strides]
+        if len(parts) > 1:
+            grams = pl.pallas_call(
+                total_kernel,
+                in_specs=[VMEM] * len(parts),
+                out_specs=VMEM,
+                out_shape=gram_type,
+                compiler_params=pltpu.CompilerParams(vmem_limit_bytes=2 << 20),
+                name="total",
+            )(*parts)
+        parts = [grams] + [exchanged(grams, axis, stride) for stride in strides]
     outs = pl.pallas_call(
         update_kernel,
         in_specs=[VMEM] * (len(parts) + 4),

time: 35.6 us -> 35 us (0.983)
  Pallas kernels: 8.21 us -> 7.61 us
    pallas_call x1, Pallas kernels: 3.26 us -> 2.53 us  [local(): pl.pallas_call(update_kernel, in_specs=[VMEM] * (len(parts) + 4), out_spe...]
    unnamed x12 -> x10, local copies, waits for them, and re-layouts: 1.46 us -> 1.4 us
  transfers between devices with their start and end apart: 13 -> 13, of which waited for: 9 -> 8; matrix products, arithmetic and copies ran while one was open for 0% -> 0% of each run, Pallas kernels for 6% -> 7%
where the time goes in v3:
time: 35 us; the launch traced here: 34.8 us
  starting transfers between devices  18.2 us (52%)
  Pallas kernels  7.61 us (22%)
  waiting for transfers between devices  6.76 us (19%)
  local copies, waits for them, and re-layouts  1.4 us (4%)
  between operations  0.73 us (2%)
    ppermute x11, starting transfers between devices, exchanged(): lax.ppermute(value, axis, [(i, i ^ stride) for i in range(lax.axis_size(a...  12.1 us
    ppermute x11, waiting for transfers between devices, exchanged(): lax.ppermute(value, axis, [(i, i ^ stride) for i in range(lax.axis_size(a...  6.74 us
    ppermute x2, starting transfers between devices, local(): lax.ppermute(dirs, 'tm', [way for i, j in pair for way in ((i, j), (j, i))])  6.13 us
    pallas_call x1, Pallas kernels, local(): pl.pallas_call(functools.partial(image_kernel, len(late)), in_specs=[SMEM...  2.77 us
    pallas_call x1, Pallas kernels, local(): pl.pallas_call(update_kernel, in_specs=[VMEM] * (len(parts) + 4), out_spe...  2.53 us
    pallas_call x1, Pallas kernels, local(): pl.pallas_call(first_kernel, in_specs=[SMEM] * 2 + [VMEM] * 4, out_specs=...  2.26 us
    unnamed x10, local copies, waits for them, and re-layouts  1.4 us
  transfers between devices with their start and end apart: 13, of which 8 were waited for; matrix products, arithmetic and copies ran while one was open for 0% of the time, Pallas kernels for 7%

profile of v3, /device:TPU:0, one launch (start us, length us, event | category | flops | bytes accessed | tf_op | source)
XLA Modules:
  0.0 34.8 jit_solution(5308614460461564028)
XLA Ops:
  0.6 0.0 copy-start.1
  0.6 0.5 %collective-permute-start = (f32[16,1024]{1,0:T(8,128)}, f32[16,1024]{1,0:T(8,128)S(1)}, u32[]{:S(2)}, u32[]{:S(2)}) collective-permute-start(f32[16,1024]{1,0:T(8,128)} %bitcast.19), channel_id=1, source_target_pairs={{0,1},{1,0},{2,3},{3,2},{4,5},{5,4},{6,7},{7,6},{8,9},{9,8},{10,11... | collective-permute-start | bytes 196616 | tf_op jit(solution)/shard_map/ppermute | solution.py:157
  1.2 0.7 %collective-permute-start.5 = (f32[16,1024]{1,0:T(8,128)}, f32[16,1024]{1,0:T(8,128)S(1)}, u32[]{:S(2)}, u32[]{:S(2)}) collective-permute-start(f32[16,1024]{1,0:T(8,128)} %bitcast.20), channel_id=1, source_target_pairs={{8,16},{16,8},{9,17},{17,9},{10,18},{18,10},{11,19},{19,11},{12,20... | collective-permute-start | bytes 196616 | tf_op jit(solution)/shard_map/ppermute | solution.py:222
  1.8 5.5 %collective-permute-start.4 = (f32[16,1024]{1,0:T(8,128)}, f32[16,1024]{1,0:T(8,128)S(1)}, u32[]{:S(2)}, u32[]{:S(2)}) collective-permute-start(f32[16,1024]{1,0:T(8,128)} %bitcast.21), channel_id=1, source_target_pairs={{0,8},{8,0},{16,24},{24,16},{1,9},{9,1},{17,25},{25,17},{2,10},{10... | collective-permute-start | bytes 196616 | tf_op jit(solution)/shard_map/ppermute | solution.py:222
  7.3 0.0 copy-start
  7.3 0.0 copy-start.2
  7.3 0.0 copy-start.4
  7.3 0.0 collective-permute-done.refs_4_
  7.3 0.0 copy-done.1
  7.4 1.6 %collective-permute-start.3 = (bf16[16,2048]{1,0:T(8,128)(2,1)S(1)}, bf16[16,2048]{1,0:T(8,128)(2,1)S(1)}, u32[]{:S(2)}, u32[]{:S(2)}) collective-permute-start(bf16[16,2048]{1,0:T(8,128)(2,1)S(1)} %place.1.block_ref), channel_id=1, source_target_pairs={{0,2},{1,3},{2,0},{3,1},{4,6},{5,7},{6,4},{7,5},{8,10},{9,11},{10,... | collective-permute-start | bytes 196616 | tf_op jit(solution)/shard_map/ppermute | solution.py:157
  8.9 1.5 %collective-permute-start.2 = (bf16[16,2048]{1,0:T(8,128)(2,1)S(1)}, bf16[16,2048]{1,0:T(8,128)(2,1)S(1)}, u32[]{:S(2)}, u32[]{:S(2)}) collective-permute-start(bf16[16,2048]{1,0:T(8,128)(2,1)S(1)} %place.1.block_ref), channel_id=1, source_target_pairs={{0,6},{1,7},{2,4},{3,5},{4,2},{5,3},{6,0},{7,1},{8,14},{9,15},{10,... | collective-permute-start | bytes 196616 | tf_op jit(solution)/shard_map/ppermute | solution.py:157
  10.4 0.5 %collective-permute-start.1 = (bf16[16,2048]{1,0:T(8,128)(2,1)S(1)}, bf16[16,2048]{1,0:T(8,128)(2,1)S(1)}, u32[]{:S(2)}, u32[]{:S(2)}) collective-permute-start(bf16[16,2048]{1,0:T(8,128)(2,1)S(1)} %place.1.block_ref), channel_id=1, source_target_pairs={{0,4},{1,5},{2,6},{3,7},{4,0},{5,1},{6,2},{7,3},{8,12},{9,13},{10,... | collective-permute-start | bytes 196616 | tf_op jit(solution)/shard_map/ppermute | solution.py:157
  10.9 0.1 pad_add_fusion._
  11.0 0.0 copy-start.3
  11.0 0.7 %collective-permute-done.3.next_ref = bf16[16,2048]{1,0:T(8,128)(2,1)S(1)} collective-permute-done((bf16[16,2048]{1,0:T(8,128)(2,1)S(1)}, bf16[16,2048]{1,0:T(8,128)(2,1)S(1)}, u32[]{:S(2)}, u32[]{:S(2)}) %collective-permute-start.3) | collective-permute-done | bytes 65568 | tf_op jit(solution)/shard_map/ppermute | solution.py:157
  11.7 1.4 %copy-done = bf16[1,1024,8192]{2,1,0:T(8,128)(2,1)S(1)} copy-done((bf16[1,1024,8192]{2,1,0:T(8,128)(2,1)S(1)}, bf16[1,1024,8192]{2,1,0:T(8,128)(2,1)}, u32[]{:S(2)}) %copy-start) | copy-done | bytes 16777240
  13.1 2.3 %first.1.refs_7_ = f32[16,1024]{1,0:T(8,128)S(1)} custom-call(s32[1]{0:T(128)} %bitcast.8.place_ref, s32[1]{0:T(128)} %bitcast.9.next_place_ref, bf16[16,2048]{1,0:T(8,128)(2,1)S(1)} %place.1.block_ref, bf16[16,2048]{1,0:T(8,128)(2,1)S(1)} %collective-permute-done.3.next_ref, bf16[1024,8192]{1,0:T(8,128)(2,1)S(1)} %bitcast.17, s32[4]{0:T(128)S(1)} %pad_add_fusion._), custom_call_target="tpu_custom_call" | custom-call | flops 67108864 | bytes 4194304 | tf_op jit(solution)/shard_map/first/pallas_call | solution.py:212
  15.3 0.0 collective-permute-done.5.refs_11_
  15.3 0.0 collective-permute-done.4.refs_10_
  15.4 0.0 collective-permute-done.2.refs_3_
  15.4 0.0 collective-permute-done.1.refs_2_
  15.4 0.0 copy-done.2
  15.4 0.0 copy-done.4
  15.4 2.8 %image.1 = (f32[16,1024]{1,0:T(8,128)S(1)}, f32[24,96]{1,0:T(8,128)S(1)}) custom-call(s32[1]{0:T(128)} %bitcast.refs_0_, s32[1]{0:T(128)} %bitcast.1.refs_1_, bf16[16,2048]{1,0:T(8,128)(2,1)S(1)} %collective-permute-done.1.refs_2_, bf16[16,2048]{1,0:T(8,128)(2,1)S(1)} %collective-permute-done.2.refs_3_, s32[1]{0:T(128)} %bitcast.6.refs_4_, ...), custom_call_target="tpu_custom_call" | custom-call | tf_op jit(solution)/shard_map/image/pallas_call | solution.py:226
  18.2 0.0 collective-permute-start.6
  18.2 1.2 %collective-permute-done.6.refs_1_ = f32[24,96]{1,0:T(8,128)S(1)} collective-permute-done((f32[24,96]{1,0:T(8,128)S(1)}, f32[24,96]{1,0:T(8,128)S(1)}, u32[]{:S(2)}, u32[]{:S(2)}) %collective-permute-start.6) | collective-permute-done | bytes 9248 | tf_op jit(solution)/shard_map/ppermute | solution.py:157
  19.4 2.5 %collective-permute-start.9 = (f32[24,96]{1,0:T(8,128)S(1)}, f32[24,96]{1,0:T(8,128)S(1)}, u32[]{:S(2)}, u32[]{:S(2)}) collective-permute-start(f32[24,96]{1,0:T(8,128)S(1)} %total.2.refs_0_), channel_id=1, source_target_pairs={{0,6},{1,7},{2,4},{3,5},{4,2},{5,3},{6,0},{7,1},{8,14},{9,15},{10,... | collective-permute-start | bytes 27656 | tf_op jit(solution)/shard_map/ppermute | solution.py:157
  21.9 0.5 %collective-permute-start.8 = (f32[24,96]{1,0:T(8,128)S(1)}, f32[24,96]{1,0:T(8,128)S(1)}, u32[]{:S(2)}, u32[]{:S(2)}) collective-permute-start(f32[24,96]{1,0:T(8,128)S(1)} %total.2.refs_0_), channel_id=1, source_target_pairs={{0,4},{1,5},{2,6},{3,7},{4,0},{5,1},{6,2},{7,3},{8,12},{9,13},{10,... | collective-permute-start | bytes 27656 | tf_op jit(solution)/shard_map/ppermute | solution.py:157
  22.4 0.5 %collective-permute-start.7 = (f32[24,96]{1,0:T(8,128)S(1)}, f32[24,96]{1,0:T(8,128)S(1)}, u32[]{:S(2)}, u32[]{:S(2)}) collective-permute-start(f32[24,96]{1,0:T(8,128)S(1)} %total.2.refs_0_), channel_id=1, source_target_pairs={{0,2},{1,3},{2,0},{3,1},{4,6},{5,7},{6,4},{7,5},{8,10},{9,11},{10,... | collective-permute-start | bytes 27656 | tf_op jit(solution)/shard_map/ppermute | solution.py:157
  22.9 1.1 %collective-permute-done.9.refs_3_ = f32[24,96]{1,0:T(8,128)S(1)} collective-permute-done((f32[24,96]{1,0:T(8,128)S(1)}, f32[24,96]{1,0:T(8,128)S(1)}, u32[]{:S(2)}, u32[]{:S(2)}) %collective-permute-start.9) | collective-permute-done | bytes 9248 | tf_op jit(solution)/shard_map/ppermute | solution.py:157
  24.0 1.5 %collective-permute-done.8.refs_2_ = f32[24,96]{1,0:T(8,128)S(1)} collective-permute-done((f32[24,96]{1,0:T(8,128)S(1)}, f32[24,96]{1,0:T(8,128)S(1)}, u32[]{:S(2)}, u32[]{:S(2)}) %collective-permute-start.8) | collective-permute-done | bytes 9248 | tf_op jit(solution)/shard_map/ppermute | solution.py:157
  25.6 0.5 %collective-permute-done.7.refs_1_ = f32[24,96]{1,0:T(8,128)S(1)} collective-permute-done((f32[24,96]{1,0:T(8,128)S(1)}, f32[24,96]{1,0:T(8,128)S(1)}, u32[]{:S(2)}, u32[]{:S(2)}) %collective-permute-start.7) | collective-permute-done | bytes 9248 | tf_op jit(solution)/shard_map/ppermute | solution.py:157
  26.1 1.4 %collective-permute-start.12 = (f32[24,96]{1,0:T(8,128)S(1)}, f32[24,96]{1,0:T(8,128)S(1)}, u32[]{:S(2)}, u32[]{:S(2)}) collective-permute-start(f32[24,96]{1,0:T(8,128)S(1)} %total.3.refs_0_), channel_id=1, source_target_pairs={{0,24},{8,16},{16,8},{24,0},{1,25},{9,17},{17,9},{25,1},{2,26},{10... | collective-permute-start | bytes 27656 | tf_op jit(solution)/shard_map/ppermute | solution.py:157
  27.5 0.2 collective-permute-start.11
  27.7 2.9 %collective-permute-start.10 = (f32[24,96]{1,0:T(8,128)S(1)}, f32[24,96]{1,0:T(8,128)S(1)}, u32[]{:S(2)}, u32[]{:S(2)}) collective-permute-start(f32[24,96]{1,0:T(8,128)S(1)} %total.3.refs_0_), channel_id=1, source_target_pairs={{0,8},{8,0},{16,24},{24,16},{1,9},{9,1},{17,25},{25,17},{2,10},{10... | collective-permute-start | bytes 27656 | tf_op jit(solution)/shard_map/ppermute | solution.py:157
  30.6 1.1 %collective-permute-done.12.refs_3_ = f32[24,96]{1,0:T(8,128)S(1)} collective-permute-done((f32[24,96]{1,0:T(8,128)S(1)}, f32[24,96]{1,0:T(8,128)S(1)}, u32[]{:S(2)}, u32[]{:S(2)}) %collective-permute-start.12) | collective-permute-done | bytes 9248 | tf_op jit(solution)/shard_map/ppermute | solution.py:157
  31.7 0.4 %collective-permute-done.11.refs_2_ = f32[24,96]{1,0:T(8,128)S(1)} collective-permute-done((f32[24,96]{1,0:T(8,128)S(1)}, f32[24,96]{1,0:T(8,128)S(1)}, u32[]{:S(2)}, u32[]{:S(2)}) %collective-permute-start.11) | collective-permute-done | bytes 9248 | tf_op jit(solution)/shard_map/ppermute | solution.py:157
  32.1 0.1 collective-permute-done.10.refs_1_
  32.3 0.0 copy-done.3
  32.3 2.5 %update.1 = (f32[16,1024]{1,0:T(8,128)}, f32[16,1024]{1,0:T(8,128)}, f32[16,1024]{1,0:T(8,128)}) custom-call(f32[24,96]{1,0:T(8,128)S(1)} %total.3.refs_0_, f32[24,96]{1,0:T(8,128)S(1)} %collective-permute-done.10.refs_1_, f32[24,96]{1,0:T(8,128)S(1)} %collective-permute-done.11.refs_2_, f32[24,96]{1,0:T(8,128)S(1)} %collective-permute-done.12.refs_3_, ...), custom_call_target="tpu_custom_call" | custom-call | tf_op jit(solution)/shard_map/update/pallas_call | solution.py:250
  (4 shorter events, 0.0 us)
Async XLA Ops:
  0.6 6.7 %copy-start.1 = (f32[1,16,1024]{2,1,0:T(8,128)S(1)}, f32[1,16,1024]{2,1,0:T(8,128)}, u32[]{:S(2)}) copy-start(f32[1,16,1024]{2,1,0:T(8,128)} %param.7) | copy-start | bytes 196612
  0.6 6.7 %collective-permute-start = (f32[16,1024]{1,0:T(8,128)}, f32[16,1024]{1,0:T(8,128)S(1)}, u32[]{:S(2)}, u32[]{:S(2)}) collective-permute-start(f32[16,1024]{1,0:T(8,128)} %bitcast.19), channel_id=1, source_target_pairs={{0,1},{1,0},{2,3},{3,2},{4,5},{5,4},{6,7},{7,6},{8,9},{9,8},{10,11... | collective-permute-start | bytes 196616 | tf_op jit(solution)/shard_map/ppermute | solution.py:157
  1.2 14.2 %collective-permute-start.5 = (f32[16,1024]{1,0:T(8,128)}, f32[16,1024]{1,0:T(8,128)S(1)}, u32[]{:S(2)}, u32[]{:S(2)}) collective-permute-start(f32[16,1024]{1,0:T(8,128)} %bitcast.20), channel_id=1, source_target_pairs={{8,16},{16,8},{9,17},{17,9},{10,18},{18,10},{11,19},{19,11},{12,20... | collective-permute-start | bytes 196616 | tf_op jit(solution)/shard_map/ppermute | solution.py:222
  1.8 13.5 %collective-permute-start.4 = (f32[16,1024]{1,0:T(8,128)}, f32[16,1024]{1,0:T(8,128)S(1)}, u32[]{:S(2)}, u32[]{:S(2)}) collective-permute-start(f32[16,1024]{1,0:T(8,128)} %bitcast.21), channel_id=1, source_target_pairs={{0,8},{8,0},{16,24},{24,16},{1,9},{9,1},{17,25},{25,17},{2,10},{10... | collective-permute-start | bytes 196616 | tf_op jit(solution)/shard_map/ppermute | solution.py:222
  7.3 5.8 %copy-start = (bf16[1,1024,8192]{2,1,0:T(8,128)(2,1)S(1)}, bf16[1,1024,8192]{2,1,0:T(8,128)(2,1)}, u32[]{:S(2)}) copy-start(bf16[1,1024,8192]{2,1,0:T(8,128)(2,1)} %param.8) | copy-start | bytes 50331652
  7.3 8.1 %copy-start.2 = (f32[1,16,1024]{2,1,0:T(8,128)S(1)}, f32[1,16,1024]{2,1,0:T(8,128)}, u32[]{:S(2)}) copy-start(f32[1,16,1024]{2,1,0:T(8,128)} %param.6) | copy-start | bytes 196612
  7.3 8.1 %copy-start.4 = (f32[1024]{0:T(1024)S(1)}, f32[1024]{0:T(1024)}, u32[]{:S(2)}) copy-start(f32[1024]{0:T(1024)} %param.9) | copy-start | bytes 12292
  7.4 4.3 %collective-permute-start.3 = (bf16[16,2048]{1,0:T(8,128)(2,1)S(1)}, bf16[16,2048]{1,0:T(8,128)(2,1)S(1)}, u32[]{:S(2)}, u32[]{:S(2)}) collective-permute-start(bf16[16,2048]{1,0:T(8,128)(2,1)S(1)} %place.1.block_ref), channel_id=1, source_target_pairs={{0,2},{1,3},{2,0},{3,1},{4,6},{5,7},{6,4},{7,5},{8,10},{9,11},{10,... | collective-permute-start | bytes 196616 | tf_op jit(solution)/shard_map/ppermute | solution.py:157
  8.9 6.5 %collective-permute-start.2 = (bf16[16,2048]{1,0:T(8,128)(2,1)S(1)}, bf16[16,2048]{1,0:T(8,128)(2,1)S(1)}, u32[]{:S(2)}, u32[]{:S(2)}) collective-permute-start(bf16[16,2048]{1,0:T(8,128)(2,1)S(1)} %place.1.block_ref), channel_id=1, source_target_pairs={{0,6},{1,7},{2,4},{3,5},{4,2},{5,3},{6,0},{7,1},{8,14},{9,15},{10,... | collective-permute-start | bytes 196616 | tf_op jit(solution)/shard_map/ppermute | solution.py:157
  10.4 5.0 %collective-permute-start.1 = (bf16[16,2048]{1,0:T(8,128)(2,1)S(1)}, bf16[16,2048]{1,0:T(8,128)(2,1)S(1)}, u32[]{:S(2)}, u32[]{:S(2)}) collective-permute-start(bf16[16,2048]{1,0:T(8,128)(2,1)S(1)} %place.1.block_ref), channel_id=1, source_target_pairs={{0,4},{1,5},{2,6},{3,7},{4,0},{5,1},{6,2},{7,3},{8,12},{9,13},{10,... | collective-permute-start | bytes 196616 | tf_op jit(solution)/shard_map/ppermute | solution.py:157
  11.0 21.3 %copy-start.3 = (f32[1,16,1024]{2,1,0:T(8,128)S(1)}, f32[1,16,1024]{2,1,0:T(8,128)}, u32[]{:S(2)}) copy-start(f32[1,16,1024]{2,1,0:T(8,128)} %param.5) | copy-start | bytes 196612
  18.2 1.2 %collective-permute-start.6 = (f32[24,96]{1,0:T(8,128)S(1)}, f32[24,96]{1,0:T(8,128)S(1)}, u32[]{:S(2)}, u32[]{:S(2)}) collective-permute-start(f32[24,96]{1,0:T(8,128)S(1)} %get-tuple-element.8.refs_0_), channel_id=1, source_target_pairs={{0,1},{1,0},{2,3},{3,2},{4,5},{5,4},{6,7},{7,6},{8,9},{9,8},{10,11... | collective-permute-start | bytes 27656 | tf_op jit(solution)/shard_map/ppermute | solution.py:157
  19.4 4.7 %collective-permute-start.9 = (f32[24,96]{1,0:T(8,128)S(1)}, f32[24,96]{1,0:T(8,128)S(1)}, u32[]{:S(2)}, u32[]{:S(2)}) collective-permute-start(f32[24,96]{1,0:T(8,128)S(1)} %total.2.refs_0_), channel_id=1, source_target_pairs={{0,6},{1,7},{2,4},{3,5},{4,2},{5,3},{6,0},{7,1},{8,14},{9,15},{10,... | collective-permute-start | bytes 27656 | tf_op jit(solution)/shard_map/ppermute | solution.py:157
  21.9 3.7 %collective-permute-start.8 = (f32[24,96]{1,0:T(8,128)S(1)}, f32[24,96]{1,0:T(8,128)S(1)}, u32[]{:S(2)}, u32[]{:S(2)}) collective-permute-start(f32[24,96]{1,0:T(8,128)S(1)} %total.2.refs_0_), channel_id=1, source_target_pairs={{0,4},{1,5},{2,6},{3,7},{4,0},{5,1},{6,2},{7,3},{8,12},{9,13},{10,... | collective-permute-start | bytes 27656 | tf_op jit(solution)/shard_map/ppermute | solution.py:157
  22.4 3.7 %collective-permute-start.7 = (f32[24,96]{1,0:T(8,128)S(1)}, f32[24,96]{1,0:T(8,128)S(1)}, u32[]{:S(2)}, u32[]{:S(2)}) collective-permute-start(f32[24,96]{1,0:T(8,128)S(1)} %total.2.refs_0_), channel_id=1, source_target_pairs={{0,2},{1,3},{2,0},{3,1},{4,6},{5,7},{6,4},{7,5},{8,10},{9,11},{10,... | collective-permute-start | bytes 27656 | tf_op jit(solution)/shard_map/ppermute | solution.py:157
  26.1 5.6 %collective-permute-start.12 = (f32[24,96]{1,0:T(8,128)S(1)}, f32[24,96]{1,0:T(8,128)S(1)}, u32[]{:S(2)}, u32[]{:S(2)}) collective-permute-start(f32[24,96]{1,0:T(8,128)S(1)} %total.3.refs_0_), channel_id=1, source_target_pairs={{0,24},{8,16},{16,8},{24,0},{1,25},{9,17},{17,9},{25,1},{2,26},{10... | collective-permute-start | bytes 27656 | tf_op jit(solution)/shard_map/ppermute | solution.py:157
  27.5 4.6 %collective-permute-start.11 = (f32[24,96]{1,0:T(8,128)S(1)}, f32[24,96]{1,0:T(8,128)S(1)}, u32[]{:S(2)}, u32[]{:S(2)}) collective-permute-start(f32[24,96]{1,0:T(8,128)S(1)} %total.3.refs_0_), channel_id=1, source_target_pairs={{0,16},{8,24},{16,0},{24,8},{1,17},{9,25},{17,1},{25,9},{2,18},{10... | collective-permute-start | bytes 27656 | tf_op jit(solution)/shard_map/ppermute | solution.py:157
  27.7 4.6 %collective-permute-start.10 = (f32[24,96]{1,0:T(8,128)S(1)}, f32[24,96]{1,0:T(8,128)S(1)}, u32[]{:S(2)}, u32[]{:S(2)}) collective-permute-start(f32[24,96]{1,0:T(8,128)S(1)} %total.3.refs_0_), channel_id=1, source_target_pairs={{0,8},{8,0},{16,24},{24,16},{1,9},{9,1},{17,25},{25,17},{2,10},{10... | collective-permute-start | bytes 27656 | tf_op jit(solution)/shard_map/ppermute | solution.py:157

commit v4 on v3

--- a/solution.py
+++ b/solution.py
@@ -157,10 +157,11 @@
     return lax.ppermute(value, axis, [(i, i ^ stride) for i in range(lax.axis_size(axis))])
 
 
-def rounds(count):
+def rounds(count, alone=0):
     bits = [1 << i for i in range((count - 1).bit_length())]
-    groups = [bits[:1]] + [bits[i : i + 2] for i in range(1, len(bits), 2)] if len(bits) % 2 else [bits[i : i + 2] for i in range(0, len(bits), 2)]
-    return [[group[0]] if len(group) == 1 else [group[0], group[1], group[0] + group[1]] for group in groups]
+    first = [bits.pop(alone)] if len(bits) % 2 else []
+    groups = [first] * len(first) + [bits[i : i + 2] for i in range(0, len(bits), 2)]
+    return [group if len(group) == 1 else [*group, sum(group)] for group in groups]
 
 
 def scalar(value):
@@ -234,7 +235,7 @@
         *places[2:], *late, scalar(has_before), scalar(has_after),
         normal[0], product, dirs, resid, before, after, weights[None],
     )
-    steps = [(axis, strides) for axis in ("row", "tm") for strides in rounds(lax.axis_size(axis))]
+    steps = [(axis, strides) for axis in ("row", "tm") for strides in rounds(lax.axis_size(axis), alone=-1)]
     parts = [grams]
     for axis, strides in steps:
         if len(parts) > 1:

time: 35 us -> 34.6 us (0.989)
  transfers between devices with their start and end apart: 13 -> 13, of which waited for: 8 -> 7; matrix products, arithmetic and copies ran while one was open for 0% -> 0% of each run, Pallas kernels for 7% -> 7%
where the time goes in v4:
time: 34.6 us; the launch traced here: 34.5 us
  starting transfers between devices  18.1 us (52%)
  Pallas kernels  7.61 us (22%)
  waiting for transfers between devices  6.49 us (19%)
  local copies, waits for them, and re-layouts  1.4 us (4%)
  between operations  0.74 us (2%)
    ppermute x11, starting transfers between devices, exchanged(): lax.ppermute(value, axis, [(i, i ^ stride) for i in range(lax.axis_size(a...  12 us
    ppermute x11, waiting for transfers between devices, exchanged(): lax.ppermute(value, axis, [(i, i ^ stride) for i in range(lax.axis_size(a...  6.48 us
    ppermute x2, starting transfers between devices, local(): lax.ppermute(dirs, 'tm', [way for i, j in pair for way in ((i, j), (j, i))])  6.13 us
    pallas_call x1, Pallas kernels, local(): pl.pallas_call(functools.partial(image_kernel, len(late)), in_specs=[SMEM...  2.77 us
    pallas_call x1, Pallas kernels, local(): pl.pallas_call(update_kernel, in_specs=[VMEM] * (len(parts) + 4), out_spe...  2.53 us
    pallas_call x1, Pallas kernels, local(): pl.pallas_call(first_kernel, in_specs=[SMEM] * 2 + [VMEM] * 4, out_specs=...  2.26 us
    unnamed x10, local copies, waits for them, and re-layouts  1.4 us
  transfers between devices with their start and end apart: 13, of which 7 were waited for; matrix products, arithmetic and copies ran while one was open for 0% of the time, Pallas kernels for 7%

profile of v4, /device:TPU:0, one launch (start us, length us, event | category | flops | bytes accessed | tf_op | source)
XLA Modules:
  0.0 34.5 jit_solution(10778605445143714613)
XLA Ops:
  0.6 0.0 copy-start.1
  0.6 0.5 %collective-permute-start = (f32[16,1024]{1,0:T(8,128)}, f32[16,1024]{1,0:T(8,128)S(1)}, u32[]{:S(2)}, u32[]{:S(2)}) collective-permute-start(f32[16,1024]{1,0:T(8,128)} %bitcast.19), channel_id=1, source_target_pairs={{0,1},{1,0},{2,3},{3,2},{4,5},{5,4},{6,7},{7,6},{8,9},{9,8},{10,11... | collective-permute-start | bytes 196616 | tf_op jit(solution)/shard_map/ppermute | solution.py:157
  1.2 0.7 %collective-permute-start.5 = (f32[16,1024]{1,0:T(8,128)}, f32[16,1024]{1,0:T(8,128)S(1)}, u32[]{:S(2)}, u32[]{:S(2)}) collective-permute-start(f32[16,1024]{1,0:T(8,128)} %bitcast.20), channel_id=1, source_target_pairs={{8,16},{16,8},{9,17},{17,9},{10,18},{18,10},{11,19},{19,11},{12,20... | collective-permute-start | bytes 196616 | tf_op jit(solution)/shard_map/ppermute | solution.py:223
  1.8 5.5 %collective-permute-start.4 = (f32[16,1024]{1,0:T(8,128)}, f32[16,1024]{1,0:T(8,128)S(1)}, u32[]{:S(2)}, u32[]{:S(2)}) collective-permute-start(f32[16,1024]{1,0:T(8,128)} %bitcast.21), channel_id=1, source_target_pairs={{0,8},{8,0},{16,24},{24,16},{1,9},{9,1},{17,25},{25,17},{2,10},{10... | collective-permute-start | bytes 196616 | tf_op jit(solution)/shard_map/ppermute | solution.py:223
  7.3 0.0 copy-start
  7.3 0.0 copy-start.2
  7.3 0.0 copy-start.4
  7.3 0.0 collective-permute-done.refs_4_
  7.3 0.0 copy-done.1
  7.4 1.6 %collective-permute-start.3 = (bf16[16,2048]{1,0:T(8,128)(2,1)S(1)}, bf16[16,2048]{1,0:T(8,128)(2,1)S(1)}, u32[]{:S(2)}, u32[]{:S(2)}) collective-permute-start(bf16[16,2048]{1,0:T(8,128)(2,1)S(1)} %place.1.block_ref), channel_id=1, source_target_pairs={{0,2},{1,3},{2,0},{3,1},{4,6},{5,7},{6,4},{7,5},{8,10},{9,11},{10,... | collective-permute-start | bytes 196616 | tf_op jit(solution)/shard_map/ppermute | solution.py:157
  8.9 1.5 %collective-permute-start.2 = (bf16[16,2048]{1,0:T(8,128)(2,1)S(1)}, bf16[16,2048]{1,0:T(8,128)(2,1)S(1)}, u32[]{:S(2)}, u32[]{:S(2)}) collective-permute-start(bf16[16,2048]{1,0:T(8,128)(2,1)S(1)} %place.1.block_ref), channel_id=1, source_target_pairs={{0,6},{1,7},{2,4},{3,5},{4,2},{5,3},{6,0},{7,1},{8,14},{9,15},{10,... | collective-permute-start | bytes 196616 | tf_op jit(solution)/shard_map/ppermute | solution.py:157
  10.4 0.5 %collective-permute-start.1 = (bf16[16,2048]{1,0:T(8,128)(2,1)S(1)}, bf16[16,2048]{1,0:T(8,128)(2,1)S(1)}, u32[]{:S(2)}, u32[]{:S(2)}) collective-permute-start(bf16[16,2048]{1,0:T(8,128)(2,1)S(1)} %place.1.block_ref), channel_id=1, source_target_pairs={{0,4},{1,5},{2,6},{3,7},{4,0},{5,1},{6,2},{7,3},{8,12},{9,13},{10,... | collective-permute-start | bytes 196616 | tf_op jit(solution)/shard_map/ppermute | solution.py:157
  10.9 0.1 pad_add_fusion._
  11.0 0.0 copy-start.3
  11.0 0.7 %collective-permute-done.3.next_ref = bf16[16,2048]{1,0:T(8,128)(2,1)S(1)} collective-permute-done((bf16[16,2048]{1,0:T(8,128)(2,1)S(1)}, bf16[16,2048]{1,0:T(8,128)(2,1)S(1)}, u32[]{:S(2)}, u32[]{:S(2)}) %collective-permute-start.3) | collective-permute-done | bytes 65568 | tf_op jit(solution)/shard_map/ppermute | solution.py:157
  11.7 1.4 %copy-done = bf16[1,1024,8192]{2,1,0:T(8,128)(2,1)S(1)} copy-done((bf16[1,1024,8192]{2,1,0:T(8,128)(2,1)S(1)}, bf16[1,1024,8192]{2,1,0:T(8,128)(2,1)}, u32[]{:S(2)}) %copy-start) | copy-done | bytes 16777240
  13.1 2.3 %first.1.refs_7_ = f32[16,1024]{1,0:T(8,128)S(1)} custom-call(s32[1]{0:T(128)} %bitcast.8.place_ref, s32[1]{0:T(128)} %bitcast.9.next_place_ref, bf16[16,2048]{1,0:T(8,128)(2,1)S(1)} %place.1.block_ref, bf16[16,2048]{1,0:T(8,128)(2,1)S(1)} %collective-permute-done.3.next_ref, bf16[1024,8192]{1,0:T(8,128)(2,1)S(1)} %bitcast.17, s32[4]{0:T(128)S(1)} %pad_add_fusion._), custom_call_target="tpu_custom_call" | custom-call | flops 67108864 | bytes 4194304 | tf_op jit(solution)/shard_map/first/pallas_call | solution.py:213
  15.3 0.0 collective-permute-done.5.refs_11_
  15.3 0.0 collective-permute-done.4.refs_10_
  15.4 0.0 collective-permute-done.2.refs_3_
  15.4 0.0 collective-permute-done.1.refs_2_
  15.4 0.0 copy-done.2
  15.4 0.0 copy-done.4
  15.4 2.8 %image.1 = (f32[16,1024]{1,0:T(8,128)S(1)}, f32[24,96]{1,0:T(8,128)S(1)}) custom-call(s32[1]{0:T(128)} %bitcast.refs_0_, s32[1]{0:T(128)} %bitcast.1.refs_1_, bf16[16,2048]{1,0:T(8,128)(2,1)S(1)} %collective-permute-done.1.refs_2_, bf16[16,2048]{1,0:T(8,128)(2,1)S(1)} %collective-permute-done.2.refs_3_, s32[1]{0:T(128)} %bitcast.6.refs_4_, ...), custom_call_target="tpu_custom_call" | custom-call | tf_op jit(solution)/shard_map/image/pallas_call | solution.py:227
  18.2 1.5 %collective-permute-start.6 = (f32[24,96]{1,0:T(8,128)S(1)}, f32[24,96]{1,0:T(8,128)S(1)}, u32[]{:S(2)}, u32[]{:S(2)}) collective-permute-start(f32[24,96]{1,0:T(8,128)S(1)} %get-tuple-element.8.refs_0_), channel_id=1, source_target_pairs={{0,4},{1,5},{2,6},{3,7},{4,0},{5,1},{6,2},{7,3},{8,12},{9,13},{10,... | collective-permute-start | bytes 27656 | tf_op jit(solution)/shard_map/ppermute | solution.py:157
  19.7 2.2 %collective-permute-done.6.refs_1_ = f32[24,96]{1,0:T(8,128)S(1)} collective-permute-done((f32[24,96]{1,0:T(8,128)S(1)}, f32[24,96]{1,0:T(8,128)S(1)}, u32[]{:S(2)}, u32[]{:S(2)}) %collective-permute-start.6) | collective-permute-done | bytes 9248 | tf_op jit(solution)/shard_map/ppermute | solution.py:157
  21.9 0.1 collective-permute-start.9
  22.0 1.6 %collective-permute-start.8 = (f32[24,96]{1,0:T(8,128)S(1)}, f32[24,96]{1,0:T(8,128)S(1)}, u32[]{:S(2)}, u32[]{:S(2)}) collective-permute-start(f32[24,96]{1,0:T(8,128)S(1)} %total.2.refs_0_), channel_id=1, source_target_pairs={{0,2},{1,3},{2,0},{3,1},{4,6},{5,7},{6,4},{7,5},{8,10},{9,11},{10,... | collective-permute-start | bytes 27656 | tf_op jit(solution)/shard_map/ppermute | solution.py:157
  23.5 0.3 collective-permute-start.7
  23.8 1.3 %collective-permute-done.9.refs_3_ = f32[24,96]{1,0:T(8,128)S(1)} collective-permute-done((f32[24,96]{1,0:T(8,128)S(1)}, f32[24,96]{1,0:T(8,128)S(1)}, u32[]{:S(2)}, u32[]{:S(2)}) %collective-permute-start.9) | collective-permute-done | bytes 9248 | tf_op jit(solution)/shard_map/ppermute | solution.py:157
  25.2 0.6 %collective-permute-done.8.refs_2_ = f32[24,96]{1,0:T(8,128)S(1)} collective-permute-done((f32[24,96]{1,0:T(8,128)S(1)}, f32[24,96]{1,0:T(8,128)S(1)}, u32[]{:S(2)}, u32[]{:S(2)}) %collective-permute-start.8) | collective-permute-done | bytes 9248 | tf_op jit(solution)/shard_map/ppermute | solution.py:157
  25.7 0.0 collective-permute-done.7.refs_1_
  25.8 1.4 %collective-permute-start.12 = (f32[24,96]{1,0:T(8,128)S(1)}, f32[24,96]{1,0:T(8,128)S(1)}, u32[]{:S(2)}, u32[]{:S(2)}) collective-permute-start(f32[24,96]{1,0:T(8,128)S(1)} %total.3.refs_0_), channel_id=1, source_target_pairs={{0,24},{8,16},{16,8},{24,0},{1,25},{9,17},{17,9},{25,1},{2,26},{10... | collective-permute-start | bytes 27656 | tf_op jit(solution)/shard_map/ppermute | solution.py:157
  27.2 0.2 collective-permute-start.11
  27.4 2.8 %collective-permute-start.10 = (f32[24,96]{1,0:T(8,128)S(1)}, f32[24,96]{1,0:T(8,128)S(1)}, u32[]{:S(2)}, u32[]{:S(2)}) collective-permute-start(f32[24,96]{1,0:T(8,128)S(1)} %total.3.refs_0_), channel_id=1, source_target_pairs={{0,8},{8,0},{16,24},{24,16},{1,9},{9,1},{17,25},{25,17},{2,10},{10... | collective-permute-start | bytes 27656 | tf_op jit(solution)/shard_map/ppermute | solution.py:157
  30.2 1.1 %collective-permute-done.12.refs_3_ = f32[24,96]{1,0:T(8,128)S(1)} collective-permute-done((f32[24,96]{1,0:T(8,128)S(1)}, f32[24,96]{1,0:T(8,128)S(1)}, u32[]{:S(2)}, u32[]{:S(2)}) %collective-permute-start.12) | collective-permute-done | bytes 9248 | tf_op jit(solution)/shard_map/ppermute | solution.py:157
  31.3 0.4 %collective-permute-done.11.refs_2_ = f32[24,96]{1,0:T(8,128)S(1)} collective-permute-done((f32[24,96]{1,0:T(8,128)S(1)}, f32[24,96]{1,0:T(8,128)S(1)}, u32[]{:S(2)}, u32[]{:S(2)}) %collective-permute-start.11) | collective-permute-done | bytes 9248 | tf_op jit(solution)/shard_map/ppermute | solution.py:157
  31.8 0.1 collective-permute-done.10.refs_1_
  31.9 0.0 copy-done.3
  31.9 2.5 %update.1 = (f32[16,1024]{1,0:T(8,128)}, f32[16,1024]{1,0:T(8,128)}, f32[16,1024]{1,0:T(8,128)}) custom-call(f32[24,96]{1,0:T(8,128)S(1)} %total.3.refs_0_, f32[24,96]{1,0:T(8,128)S(1)} %collective-permute-done.10.refs_1_, f32[24,96]{1,0:T(8,128)S(1)} %collective-permute-done.11.refs_2_, f32[24,96]{1,0:T(8,128)S(1)} %collective-permute-done.12.refs_3_, ...), custom_call_target="tpu_custom_call" | custom-call | tf_op jit(solution)/shard_map/update/pallas_call | solution.py:251
  (4 shorter events, 0.0 us)
Async XLA Ops:
  0.6 6.7 %copy-start.1 = (f32[1,16,1024]{2,1,0:T(8,128)S(1)}, f32[1,16,1024]{2,1,0:T(8,128)}, u32[]{:S(2)}) copy-start(f32[1,16,1024]{2,1,0:T(8,128)} %param.7) | copy-start | bytes 196612
  0.6 6.7 %collective-permute-start = (f32[16,1024]{1,0:T(8,128)}, f32[16,1024]{1,0:T(8,128)S(1)}, u32[]{:S(2)}, u32[]{:S(2)}) collective-permute-start(f32[16,1024]{1,0:T(8,128)} %bitcast.19), channel_id=1, source_target_pairs={{0,1},{1,0},{2,3},{3,2},{4,5},{5,4},{6,7},{7,6},{8,9},{9,8},{10,11... | collective-permute-start | bytes 196616 | tf_op jit(solution)/shard_map/ppermute | solution.py:157
  1.2 14.2 %collective-permute-start.5 = (f32[16,1024]{1,0:T(8,128)}, f32[16,1024]{1,0:T(8,128)S(1)}, u32[]{:S(2)}, u32[]{:S(2)}) collective-permute-start(f32[16,1024]{1,0:T(8,128)} %bitcast.20), channel_id=1, source_target_pairs={{8,16},{16,8},{9,17},{17,9},{10,18},{18,10},{11,19},{19,11},{12,20... | collective-permute-start | bytes 196616 | tf_op jit(solution)/shard_map/ppermute | solution.py:223
  1.8 13.5 %collective-permute-start.4 = (f32[16,1024]{1,0:T(8,128)}, f32[16,1024]{1,0:T(8,128)S(1)}, u32[]{:S(2)}, u32[]{:S(2)}) collective-permute-start(f32[16,1024]{1,0:T(8,128)} %bitcast.21), channel_id=1, source_target_pairs={{0,8},{8,0},{16,24},{24,16},{1,9},{9,1},{17,25},{25,17},{2,10},{10... | collective-permute-start | bytes 196616 | tf_op jit(solution)/shard_map/ppermute | solution.py:223
  7.3 5.8 %copy-start = (bf16[1,1024,8192]{2,1,0:T(8,128)(2,1)S(1)}, bf16[1,1024,8192]{2,1,0:T(8,128)(2,1)}, u32[]{:S(2)}) copy-start(bf16[1,1024,8192]{2,1,0:T(8,128)(2,1)} %param.8) | copy-start | bytes 50331652
  7.3 8.1 %copy-start.2 = (f32[1,16,1024]{2,1,0:T(8,128)S(1)}, f32[1,16,1024]{2,1,0:T(8,128)}, u32[]{:S(2)}) copy-start(f32[1,16,1024]{2,1,0:T(8,128)} %param.6) | copy-start | bytes 196612
  7.3 8.1 %copy-start.4 = (f32[1024]{0:T(1024)S(1)}, f32[1024]{0:T(1024)}, u32[]{:S(2)}) copy-start(f32[1024]{0:T(1024)} %param.9) | copy-start | bytes 12292
  7.4 4.3 %collective-permute-start.3 = (bf16[16,2048]{1,0:T(8,128)(2,1)S(1)}, bf16[16,2048]{1,0:T(8,128)(2,1)S(1)}, u32[]{:S(2)}, u32[]{:S(2)}) collective-permute-start(bf16[16,2048]{1,0:T(8,128)(2,1)S(1)} %place.1.block_ref), channel_id=1, source_target_pairs={{0,2},{1,3},{2,0},{3,1},{4,6},{5,7},{6,4},{7,5},{8,10},{9,11},{10,... | collective-permute-start | bytes 196616 | tf_op jit(solution)/shard_map/ppermute | solution.py:157
  8.9 6.5 %collective-permute-start.2 = (bf16[16,2048]{1,0:T(8,128)(2,1)S(1)}, bf16[16,2048]{1,0:T(8,128)(2,1)S(1)}, u32[]{:S(2)}, u32[]{:S(2)}) collective-permute-start(bf16[16,2048]{1,0:T(8,128)(2,1)S(1)} %place.1.block_ref), channel_id=1, source_target_pairs={{0,6},{1,7},{2,4},{3,5},{4,2},{5,3},{6,0},{7,1},{8,14},{9,15},{10,... | collective-permute-start | bytes 196616 | tf_op jit(solution)/shard_map/ppermute | solution.py:157
  10.4 5.0 %collective-permute-start.1 = (bf16[16,2048]{1,0:T(8,128)(2,1)S(1)}, bf16[16,2048]{1,0:T(8,128)(2,1)S(1)}, u32[]{:S(2)}, u32[]{:S(2)}) collective-permute-start(bf16[16,2048]{1,0:T(8,128)(2,1)S(1)} %place.1.block_ref), channel_id=1, source_target_pairs={{0,4},{1,5},{2,6},{3,7},{4,0},{5,1},{6,2},{7,3},{8,12},{9,13},{10,... | collective-permute-start | bytes 196616 | tf_op jit(solution)/shard_map/ppermute | solution.py:157
  11.0 20.9 %copy-start.3 = (f32[1,16,1024]{2,1,0:T(8,128)S(1)}, f32[1,16,1024]{2,1,0:T(8,128)}, u32[]{:S(2)}) copy-start(f32[1,16,1024]{2,1,0:T(8,128)} %param.5) | copy-start | bytes 196612
  18.2 3.7 %collective-permute-start.6 = (f32[24,96]{1,0:T(8,128)S(1)}, f32[24,96]{1,0:T(8,128)S(1)}, u32[]{:S(2)}, u32[]{:S(2)}) collective-permute-start(f32[24,96]{1,0:T(8,128)S(1)} %get-tuple-element.8.refs_0_), channel_id=1, source_target_pairs={{0,4},{1,5},{2,6},{3,7},{4,0},{5,1},{6,2},{7,3},{8,12},{9,13},{10,... | collective-permute-start | bytes 27656 | tf_op jit(solution)/shard_map/ppermute | solution.py:157
  21.9 3.3 %collective-permute-start.9 = (f32[24,96]{1,0:T(8,128)S(1)}, f32[24,96]{1,0:T(8,128)S(1)}, u32[]{:S(2)}, u32[]{:S(2)}) collective-permute-start(f32[24,96]{1,0:T(8,128)S(1)} %total.2.refs_0_), channel_id=1, source_target_pairs={{0,3},{1,2},{2,1},{3,0},{4,7},{5,6},{6,5},{7,4},{8,11},{9,10},{10,... | collective-permute-start | bytes 27656 | tf_op jit(solution)/shard_map/ppermute | solution.py:157
  22.0 3.8 %collective-permute-start.8 = (f32[24,96]{1,0:T(8,128)S(1)}, f32[24,96]{1,0:T(8,128)S(1)}, u32[]{:S(2)}, u32[]{:S(2)}) collective-permute-start(f32[24,96]{1,0:T(8,128)S(1)} %total.2.refs_0_), channel_id=1, source_target_pairs={{0,2},{1,3},{2,0},{3,1},{4,6},{5,7},{6,4},{7,5},{8,10},{9,11},{10,... | collective-permute-start | bytes 27656 | tf_op jit(solution)/shard_map/ppermute | solution.py:157
  23.5 2.2 %collective-permute-start.7 = (f32[24,96]{1,0:T(8,128)S(1)}, f32[24,96]{1,0:T(8,128)S(1)}, u32[]{:S(2)}, u32[]{:S(2)}) collective-permute-start(f32[24,96]{1,0:T(8,128)S(1)} %total.2.refs_0_), channel_id=1, source_target_pairs={{0,1},{1,0},{2,3},{3,2},{4,5},{5,4},{6,7},{7,6},{8,9},{9,8},{10,11... | collective-permute-start | bytes 27656 | tf_op jit(solution)/shard_map/ppermute | solution.py:157
  25.8 5.6 %collective-permute-start.12 = (f32[24,96]{1,0:T(8,128)S(1)}, f32[24,96]{1,0:T(8,128)S(1)}, u32[]{:S(2)}, u32[]{:S(2)}) collective-permute-start(f32[24,96]{1,0:T(8,128)S(1)} %total.3.refs_0_), channel_id=1, source_target_pairs={{0,24},{8,16},{16,8},{24,0},{1,25},{9,17},{17,9},{25,1},{2,26},{10... | collective-permute-start | bytes 27656 | tf_op jit(solution)/shard_map/ppermute | solution.py:157
  27.2 4.6 %collective-permute-start.11 = (f32[24,96]{1,0:T(8,128)S(1)}, f32[24,96]{1,0:T(8,128)S(1)}, u32[]{:S(2)}, u32[]{:S(2)}) collective-permute-start(f32[24,96]{1,0:T(8,128)S(1)} %total.3.refs_0_), channel_id=1, source_target_pairs={{0,16},{8,24},{16,0},{24,8},{1,17},{9,25},{17,1},{25,9},{2,18},{10... | collective-permute-start | bytes 27656 | tf_op jit(solution)/shard_map/ppermute | solution.py:157
  27.4 4.5 %collective-permute-start.10 = (f32[24,96]{1,0:T(8,128)S(1)}, f32[24,96]{1,0:T(8,128)S(1)}, u32[]{:S(2)}, u32[]{:S(2)}) collective-permute-start(f32[24,96]{1,0:T(8,128)S(1)} %total.3.refs_0_), channel_id=1, source_target_pairs={{0,8},{8,0},{16,24},{24,16},{1,9},{9,1},{17,25},{25,17},{2,10},{10... | collective-permute-start | bytes 27656 | tf_op jit(solution)/shard_map/ppermute | solution.py:157
